TPU v7x, 256 devices: a whole 4x4x8 slice. The times are simulated.
256 devices in a mesh: dp: 8 (over x_lo, y), ctx: 32 (over z, x_hi, core).
Axes of the slice: x: 4 (x_hi: 2, x_lo: 2; x = x_hi * 2 + x_lo), y: 4, z: 8, core: 2. Of those that a mesh axis runs over, the one named last changes fastest.
Arguments:
- queries: bfloat16 [65536, 128], P(('dp', 'ctx')), parts along dimension 0, may hold values from -6 to 6
- key_rows: bfloat16 [65536, 128], P(('dp', 'ctx')), parts along dimension 0, may hold values from -6 to 6
- value_rows: bfloat16 [65536, 128], P(('dp', 'ctx')), parts along dimension 0, may hold values from -0.5 to 0.5
- out_grad: bfloat16 [65536, 128], P(('dp', 'ctx')), parts along dimension 0, may hold values from -6 to 6
Outputs:
- query_grad: float32 [65536, 128], P(('dp', 'ctx')), parts along dimension 0
- key_grad: float32 [65536, 128], P(('dp', 'ctx')), parts along dimension 0
- value_grad: float32 [65536, 128], P(('dp', 'ctx')), parts along dimension 0
There are 8 independent parts, one for each index of `dp`. A program takes and returns all parts, laid end to end along the dimension named above; each array names one. Nothing has to cross between parts.
All inputs are finite; a program needn't handle non-finite values.
Results may differ from a plain program's by a relative error of at most 0.0069.
Values may be sent and summed in bfloat16 or wider, within the bound.
A program may use at most 64 MiB of HBM per device.

v0:
```python
import jax
import jax.numpy as jnp
from jax import lax
from jax.sharding import PartitionSpec as P


def side_by_side(arrays, axis, dim, along):
    widths = [a.shape[along] for a in arrays]
    both = jnp.concatenate(arrays, axis=along)
    whole = lax.all_gather(both, axis, axis=dim, tiled=True)
    return tuple(jnp.split(whole, [sum(widths[:k]) for k in range(1, len(widths))], axis=along))


def joined_along(pieces, dim):
    pieces = jnp.moveaxis(pieces, 0, dim)
    shape = pieces.shape
    return pieces.reshape(*shape[:dim], shape[dim] * shape[dim + 1], *shape[dim + 2 :])


def copy_for_each(shard, axis):
    size = lax.axis_size(axis)
    return lax.all_to_all(
        jnp.broadcast_to(shard[None], (size, *shard.shape)), axis, 0, 0, tiled=True
    )


def gather_directly(shard, axis, dim):
    return joined_along(copy_for_each(shard, axis), dim)


def dot_rows(left, right):
    return lax.dot_general(
        left, right, (((1,), (1,)), ((), ())), preferred_element_type=jnp.float32
    )


def dot_cols(left, right):
    return lax.dot_general(
        left, right, (((0,), (0,)), ((), ())), preferred_element_type=jnp.float32
    )


def in_blocks(block_step, carried, pieces, offset):
    length = pieces[0].shape[0]
    block_len = length
    while block_len > 1536 and block_len % 2 == 0:
        block_len = block_len // 2

    def turn(block_index, inner):
        place = block_index * block_len
        parts = tuple((lax.dynamic_slice_in_dim(piece, place, block_len, 0) for piece in pieces))
        return block_step(inner, parts, offset + place)

    return lax.fori_loop(0, length // block_len, turn, carried)


def tile_grads(query_part, grad_part, key_part, value_part, log_part, delta_part, score_scale):
    scores = dot_rows(query_part, key_part) * score_scale
    probs = jnp.exp(scores - log_part[:, None])
    prob_grad = dot_rows(grad_part, value_part)
    score_grad = (probs * (prob_grad - delta_part[:, None])).astype(jnp.bfloat16)
    return (score_grad, probs.astype(jnp.bfloat16))


def shards(queries, key_rows, value_rows, out_grad):
    local_rows, head_width = queries.shape
    score_scale = head_width ** (-0.5)

    def stats_step(carried, pieces, offset):
        row_peak, row_total, weighted = carried
        key_part, value_part = pieces
        scores = dot_rows(queries, key_part) * score_scale
        prob_grad = dot_rows(out_grad, value_part)
        new_peak = jnp.maximum(row_peak, jnp.max(scores, axis=1))
        rescale = jnp.exp(row_peak - new_peak)
        weights_now = jnp.exp(scores - new_peak[:, None])
        row_total = row_total * rescale + jnp.sum(weights_now, axis=1)
        weighted = weighted * rescale + jnp.sum(weights_now * prob_grad, axis=1)
        return (new_peak, row_total, weighted)

    initial = (
        jnp.full((local_rows,), -1e30, jnp.float32),
        jnp.zeros((local_rows,), jnp.float32),
        jnp.zeros((local_rows,), jnp.float32),
    )
    all_keys, all_values = side_by_side((key_rows, value_rows), "ctx", 0, 1)
    row_peak, row_total, weighted = in_blocks(stats_step, initial, (all_keys, all_values), 0)
    log_total = row_peak + jnp.log(row_total)
    delta = weighted / row_total
    zero_rows = jnp.zeros((local_rows, head_width), jnp.float32)

    def query_step(carried, pieces, offset):
        key_part, value_part = pieces
        score_grad, prob_half = tile_grads(
            queries, out_grad, key_part, value_part, log_total, delta, score_scale
        )
        return carried + jnp.dot(score_grad, key_part, preferred_element_type=jnp.float32)

    query_grad = in_blocks(query_step, zero_rows, (all_keys, all_values), 0)
    all_log, all_delta = (gather_directly(log_total, "ctx", 0), gather_directly(delta, "ctx", 0))

    def key_step(carried, pieces, offset):
        key_grad, value_grad = carried
        query_part, grad_part = pieces
        length = query_part.shape[0]
        log_part = lax.dynamic_slice_in_dim(all_log, offset, length, 0)
        delta_part = lax.dynamic_slice_in_dim(all_delta, offset, length, 0)
        score_grad, prob_half = tile_grads(
            query_part, grad_part, key_rows, value_rows, log_part, delta_part, score_scale
        )
        key_grad = key_grad + dot_cols(score_grad, query_part)
        value_grad = value_grad + dot_cols(prob_half, grad_part)
        return (key_grad, value_grad)

    key_grad, value_grad = in_blocks(
        key_step,
        (zero_rows, zero_rows),
        side_by_side((queries, out_grad), "ctx", 0, 1),
        jnp.int32(0),
    )
    key_grad = key_grad * score_scale
    return (query_grad * score_scale, key_grad, value_grad)


def solution(mesh):
    in_specs = (
        P(("dp", "ctx"), None),
        P(("dp", "ctx"), None),
        P(("dp", "ctx"), None),
        P(("dp", "ctx"), None),
    )
    out_specs = (P(("dp", "ctx"), None), P(("dp", "ctx"), None), P(("dp", "ctx"), None))
    return jax.shard_map(shards, mesh=mesh, in_specs=in_specs, out_specs=out_specs, check_vma=False)
```

profile of v0, /device:TPU:1, one launch (start us, length us, event | category | flops | bytes accessed | tf_op | source)
XLA Modules:
  0.0 245.3 jit_solution(5601059789293627701)
XLA Ops:
  7.2 1.5 pad_maximum_fusion
  8.8 1.5 pad_maximum_fusion.1
  10.5 91.9 %all-gather.3.cloned.1.call-done = bf16[8192,256]{1,0:T(8,128)(2,1)} async-done(((bf16[256,256]{1,0:T(8,128)(2,1)}), bf16[8192,256]{1,0:T(8,128)(2,1)}) %all-gather.3.cloned.1.call-update) | async-done | bytes 4194320 | tf_op jit(solution)/shard_map/all_gather | solution.py:10
  102.4 3.9 %fusion.42 = (bf16[8192,128]{1,0:T(8,128)(2,1)}, bf16[8192,128]{1,0:T(8,128)(2,1)S(1)}) fusion(bf16[8192,256]{1,0:T(8,128)(2,1)} %all-gather.3.cloned.1.call-done), kind=kLoop, calls=%fused_computation.55 | loop fusion | bytes 8388608 | tf_op jit(solution)/shard_map/split | solution.py:11
  106.3 15.8 %while.48 = (s32[]{:T(128)}, f32[256]{0:T(256)S(1)}, f32[256]{0:T(256)S(1)}, f32[256]{0:T(256)S(1)}, bf16[8192,128]{1,0:T(8,128)(2,1)S(1)}, /*index=5*/bf16[256,...) while((s32[]{:T(128)}, f32[256]{0:T(256)S(1)}, ...), condition=%wide.region_4.0_spmd.clone, body=%wide.region_0.0_spmd.clone.sunk | while | flops 136054528 | bytes 3819702 | solution.py:54
  106.9 1.3 fusion.79
  108.9 1.3 fusion.79
  110.8 1.3 fusion.79
  112.8 1.3 fusion.79
  114.8 1.3 fusion.79
  116.8 1.3 fusion.79
  118.7 1.3 fusion.79
  120.7 1.3 fusion.79
  124.0 4.7 %all-to-all-start = ((f32[32,1,256]{2,1,0:T(1,128)}), f32[32,1,256]{2,1,0:T(1,128)}, u32[]{:S(2)}, u32[]{:S(2)}) async-start(f32[32,1,256]{2,1,0:T(1,128)} %broadcast_in_dim.35), calls=%async_computation | async-start | bytes 65536 | tf_op jit(solution)/shard_map/all_to_all | solution.py:22
  128.6 15.7 %while.49 = (s32[]{:T(128)}, f32[256,128]{1,0:T(8,128)S(1)}, bf16[8192,128]{1,0:T(8,128)(2,1)S(1)}, bf16[256,128]{1,0:T(8,128)(2,1)S(1)}, f32[256]{0:T(256)S(1)}...) while((s32[]{:T(128)}, f32[256,128]{1,0:T(8,128)S(1)}, ...), condition=%wide.region_6.0_spmd.clone, body=%wide.region_5.0_spmd.clone.sunk | while | flops 202702848 | bytes 3280560 | solution.py:54
  129.0 1.6 fusion.88
  130.9 1.6 fusion.88
  132.9 1.6 fusion.88
  134.9 1.6 fusion.88
  136.8 1.6 fusion.88
  138.8 1.6 fusion.88
  140.8 1.6 fusion.88
  142.7 1.6 fusion.88
  145.0 9.8 %all-to-all-start.1 = ((f32[32,1,256]{2,1,0:T(1,128)}), f32[32,1,256]{2,1,0:T(1,128)}, u32[]{:S(2)}, u32[]{:S(2)}) async-start(f32[32,1,256]{2,1,0:T(1,128)} %broadcast_in_dim.36), calls=%async_computation.1 | async-start | bytes 65536 | tf_op jit(solution)/shard_map/all_to_all | solution.py:22
  154.9 34.8 %all-gather.5.cloned.1.call-done = bf16[8192,256]{1,0:T(8,128)(2,1)} async-done(((bf16[256,256]{1,0:T(8,128)(2,1)}), bf16[8192,256]{1,0:T(8,128)(2,1)}) %all-gather.5.cloned.1.call-update) | async-done | bytes 4194320 | tf_op jit(solution)/shard_map/all_gather | solution.py:10
  189.7 3.8 %fusion.41 = (bf16[8192,128]{1,0:T(8,128)(2,1)}, bf16[8192,128]{1,0:T(8,128)(2,1)S(1)}) fusion(bf16[8192,256]{1,0:T(8,128)(2,1)} %all-gather.5.cloned.1.call-done), kind=kLoop, calls=%fused_computation.54 | loop fusion | bytes 8388608 | tf_op jit(solution)/shard_map/split | solution.py:11
  193.5 44.2 %while.50 = (s32[]{:T(128)}, f32[256,128]{1,0:T(8,128)S(1)}, f32[256,128]{1,0:T(8,128)S(1)}, bf16[8192,128]{1,0:T(8,128)(2,1)S(1)}, bf16[256,128]{1,0:T(8,128)(2...) while((s32[]{:T(128)}, f32[256,128]{1,0:T(8,128)S(1)}, ...), condition=%wide.region_8.0_spmd.clone, body=%wide.region_7.0_spmd.clone.sunk | while | flops 270139392 | bytes 4875973 | solution.py:54
  194.2 1.2 fusion.96
  195.4 1.3 convolution_add_fusion.2
  197.4 1.6 fusion.97
  199.7 1.2 fusion.96
  200.9 1.3 convolution_add_fusion.2
  202.9 1.6 fusion.97
  205.3 1.2 fusion.96
  206.5 1.3 convolution_add_fusion.2
  208.5 1.6 fusion.97
  210.8 1.2 fusion.96
  212.0 1.3 convolution_add_fusion.2
  214.0 1.6 fusion.97
  217.5 1.3 convolution_add_fusion.2
  219.5 1.6 fusion.97
  221.8 1.2 fusion.96
  223.0 1.3 convolution_add_fusion.2
  225.0 1.6 fusion.97
  228.5 1.3 convolution_add_fusion.2
  230.5 1.6 fusion.97
  234.1 1.3 convolution_add_fusion.2
  236.1 1.6 fusion.97
  (93 shorter events, 25.0 us)
Async XLA Ops:
  7.2 95.2 %all-gather.3.cloned.1.call-start = ((), (), s32[]{:S(2)}) async-start(), calls=%async_computation.2 | async-start | bytes 4325376 | tf_op jit(solution)/shard_map/all_gather | solution.py:10
  8.8 180.9 %all-gather.5.cloned.1.call-start = ((), (), s32[]{:S(2)}) async-start(), calls=%async_computation.3 | async-start | bytes 4325376 | tf_op jit(solution)/shard_map/all_gather | solution.py:10
  10.5 95.8 %copy-start = (bf16[256,128]{1,0:T(8,128)(2,1)S(1)}, bf16[256,128]{1,0:T(8,128)(2,1)}, u32[]{:S(2)}) copy-start(bf16[256,128]{1,0:T(8,128)(2,1)} %param.13) | copy-start | bytes 196612
  10.5 95.8 %copy-start.1 = (bf16[256,128]{1,0:T(8,128)(2,1)S(1)}, bf16[256,128]{1,0:T(8,128)(2,1)}, u32[]{:S(2)}) copy-start(bf16[256,128]{1,0:T(8,128)(2,1)} %param.10) | copy-start | bytes 196612
  122.1 0.6 copy-start.4
  124.0 20.4 %all-to-all-start = ((f32[32,1,256]{2,1,0:T(1,128)}), f32[32,1,256]{2,1,0:T(1,128)}, u32[]{:S(2)}, u32[]{:S(2)}) async-start(f32[32,1,256]{2,1,0:T(1,128)} %broadcast_in_dim.35), calls=%async_computation | async-start | bytes 65536 | tf_op jit(solution)/shard_map/all_to_all | solution.py:22
  145.0 48.5 %all-to-all-start.1 = ((f32[32,1,256]{2,1,0:T(1,128)}), f32[32,1,256]{2,1,0:T(1,128)}, u32[]{:S(2)}, u32[]{:S(2)}) async-start(f32[32,1,256]{2,1,0:T(1,128)} %broadcast_in_dim.36), calls=%async_computation.1 | async-start | bytes 65536 | tf_op jit(solution)/shard_map/all_to_all | solution.py:22
  154.8 38.7 %copy-start.2 = (f32[256,128]{1,0:T(8,128)S(1)}, f32[256,128]{1,0:T(8,128)}, u32[]{:S(2)}) copy-start(f32[256,128]{1,0:T(8,128)} %custom-call.5) | copy-start | bytes 393220
  237.7 0.7 copy-start.3
Sparse Core Ops, SparseCore 0:
  11.4 91.0 all-gather.2
  105.8 83.8 all-gather.4
where the time goes:
time: 247 us; the launch traced here: 245 us
  waiting for transfers between devices  127 us (51%)
  matrix products  61.7 us (25%)
  local copies, waits for them, and re-layouts  20.5 us (8%)
  starting transfers between devices  14.6 us (6%)
  between operations  14.2 us (6%)
  other arithmetic  6.49 us (3%)
    all_gather x2, waiting for transfers between devices, side_by_side(): whole = lax.all_gather(both, axis, axis=dim, tiled=True)  127 us
    dot_general x32, matrix products, dot_rows(): lax.dot_general(left, right, (((1,), (1,)), ((), ())), preferred_element_...  25.2 us
    dot_general x16, matrix products, dot_cols(): lax.dot_general(left, right, (((0,), (0,)), ((), ())), preferred_element_...  23.6 us
    all_to_all x2, starting transfers between devices, copy_for_each(): lax.all_to_all(jnp.broadcast_to(shard[None], (size, *shard.shape)), axis,...  14.5 us
    dot_general x8, matrix products, query_step(): jnp.dot(score_grad, key_part, preferred_element_type=jnp.float32)  12.9 us
    split x2, local copies, waits for them, and re-layouts, side_by_side(): jnp.split(whole, [sum(widths[:k]) for k in range(1, len(widths))], axis=a...  7.7 us
    dynamic_slice x8, local copies, waits for them, and re-layouts, key_step(): log_part = lax.dynamic_slice_in_dim(all_log, offset, length, 0)  5.46 us
    dynamic_slice x8, local copies, waits for them, and re-layouts, key_step(): delta_part = lax.dynamic_slice_in_dim(all_delta, offset, length, 0)  5.44 us
  transfers between devices with their start and end apart: 4, of which 2 were waited for; matrix products, arithmetic and copies ran while one was open for 17% of the time, Pallas kernels for 0%

commit v1 on v0

v1 whole, which is shorter than its diff:
```python
import math

import jax
import jax.numpy as jnp
from jax import lax
from jax.experimental import pallas as pl
from jax.experimental.pallas import tpu as pltpu
from jax.sharding import PartitionSpec as P

F32 = jnp.float32
BF16 = jnp.bfloat16
MESH = pl.DeviceIdType.MESH

ROWS = 256
WIDTH = 128
RING = 8
HALF = 512
KEYS = 1024
SCALE = WIDTH ** (-0.5)
EXP2_SCALE = SCALE * math.log2(math.e)

OWN, FAR, R1, L1, R2, L2, R3, L3 = range(8)
PLACE = (0, 4, -1, 1, -2, 2, -3, 3)
MIRROR = (OWN, FAR, L1, R1, L2, R2, L3, R3)


def rows_dot(left, right):
    return lax.dot_general(left, right, (((1,), (1,)), ((), ())), preferred_element_type=F32)


def kernel(
    q_hbm, k_hbm, v_hbm, g_hbm,
    dq_hbm, dk_hbm, dv_hbm,
    qbuf, gbuf, kbuf, vbuf, ktbuf, ebuf, dbuf, mbuf,
    part_tx, part_rx, fin, dk_acc, dv_acc,
    dqt, dq_tx, dq_rx, pair_tx, pair_rx, far_tx, far_rx, out_buf,
    in_sem, gat_send, gat_recv, kv_send, kv_recv, st_send, st_recv, fin_send, fin_recv,
    dq_send, dq_recv, red_send, red_recv, out_sem,
):
    me = lax.axis_index("ctx")
    z = me // 4
    w = me % 4
    core = w % 2
    xh = w // 2

    def on_ring(offset):
        return {"ctx": ((z + (offset + RING)) % RING) * 4 + w}

    sibling = {"ctx": z * 4 + xh * 2 + (1 - core)}
    across = {"ctx": z * 4 + (1 - xh) * 2 + core}

    barrier = pltpu.get_barrier_semaphore()
    for peer in [on_ring(PLACE[s]) for s in range(1, 8)] + [sibling, across]:
        pl.semaphore_signal(barrier, inc=1, device_id=peer, device_id_type=MESH)

    own_rows = pl.ds(0, ROWS)
    loads = [
        pltpu.make_async_copy(src, dst, in_sem.at[i])
        for i, (src, dst) in enumerate(
            (
                (q_hbm, qbuf.at[OWN]),
                (g_hbm, gbuf.at[OWN]),
                (k_hbm, kbuf.at[own_rows]),
                (v_hbm, vbuf.at[own_rows]),
            )
        )
    ]
    for c in loads:
        c.start()
    pending = []

    def send(src, dst, send_sem, recv_sem, peer):
        c = pltpu.make_async_remote_copy(
            src_ref=src, dst_ref=dst, send_sem=send_sem, recv_sem=recv_sem,
            device_id=peer, device_id_type=MESH,
        )
        c.start()
        pending.append(c)
        return c

    for c in loads:
        c.wait()
    pl.semaphore_wait(barrier, 9)

    right, left = on_ring(1), on_ring(-1)

    bufs = (qbuf, gbuf)

    def hop(b, d, i):
        slots = ((OWN, R1, R2, R3, FAR), (OWN, L1, L2, L3, FAR))[d]
        n = (b * 2 + d) * 4 + i
        return send(
            bufs[b].at[slots[i]], bufs[b].at[slots[i + 1]],
            gat_send.at[n], gat_recv.at[n], (right, left)[d],
        )

    def key_rows_at(p):
        return pl.ds(p * ROWS, ROWS)

    hops = {}
    for b in (0, 1):
        for d in (0, 1):
            hops[b, d, 0] = hop(b, d, 0)
    kv_across = []
    for i, buf in enumerate((kbuf, vbuf)):
        kv_across.append(
            send(buf.at[key_rows_at(0)], buf.at[key_rows_at(2)], kv_send.at[i], kv_recv.at[i], across)
        )
    kv_sibling = []
    for i, buf in enumerate((kbuf, vbuf)):
        kv_sibling.append(
            send(buf.at[key_rows_at(0)], buf.at[key_rows_at(1)], kv_send.at[2 + i], kv_recv.at[2 + i], sibling)
        )
    kv_third = []

    def pass_keys_on():
        for i, buf in enumerate((kbuf, vbuf)):
            kv_across[i].wait_recv()
            kv_third.append(
                send(buf.at[key_rows_at(2)], buf.at[key_rows_at(3)], kv_send.at[4 + i], kv_recv.at[4 + i], sibling)
            )

    def tile(slot, kh):
        keys = pl.ds(kh * HALF, HALF)
        s = rows_dot(kbuf[keys, :], qbuf[slot])
        m = jnp.max(s, axis=0, keepdims=True)
        e = jnp.exp2((s - m) * EXP2_SCALE)
        ebuf[slot, keys, :] = e
        d = rows_dot(vbuf[keys, :], gbuf[slot])
        dbuf[slot, keys, :] = d
        mbuf[slot, kh, 0:1, :] = m * SCALE
        mbuf[slot, kh, 1:2, :] = jnp.sum(e, axis=0, keepdims=True)
        mbuf[slot, kh, 2:3, :] = jnp.sum(e * d, axis=0, keepdims=True)

    def put_stats(ref, log_total, delta):
        for i in range(2):
            cols = slice(i * 128, (i + 1) * 128)
            ref[i : i + 1, :] = log_total[:, cols]
            ref[2 + i : 3 + i, :] = delta[:, cols]

    st = {}

    def stats(slot):
        m0, l0, w0 = (mbuf[slot, 0, i : i + 1, :] for i in range(3))
        m1, l1, w1 = (mbuf[slot, 1, i : i + 1, :] for i in range(3))
        m = jnp.maximum(m0, m1)
        a0, a1 = jnp.exp(m0 - m), jnp.exp(m1 - m)
        total = l0 * a0 + l1 * a1
        put_stats(part_tx.at[slot], m + jnp.log(total), (w0 * a0 + w1 * a1) / total)
        if slot != OWN:
            at = MIRROR[slot]
            st[slot] = send(
                part_tx.at[slot], part_rx.at[at], st_send.at[slot], st_recv.at[at], on_ring(PLACE[slot])
            )

    def wait_gather(b, i):
        hops[b, 0, i].wait_recv()
        if i < 3 or b == 0:
            pass

    def arrive(b, i):
        for d in (0, 1):
            hops[b, d, i].wait_recv()
            if i < 2 or b == d:
                hops[b, d, i + 1] = hop(b, d, i + 1)

    for c in kv_sibling:
        c.wait_recv()
    tile(OWN, 0)
    arrive(0, 0)
    arrive(1, 0)
    tile(R1, 0)
    tile(L1, 0)
    pass_keys_on()
    arrive(0, 1)
    for c in kv_third:
        c.wait_recv()
    for p in range(4):
        ktbuf[:, p * ROWS : (p + 1) * ROWS] = kbuf[key_rows_at(p), :].astype(F32).T.astype(BF16)
    tile(OWN, 1)
    stats(OWN)
    arrive(1, 1)
    for slot in (R1, L1):
        tile(slot, 1)
        stats(slot)
    for slot in (R2, L2):
        tile(slot, 0)
        tile(slot, 1)
        stats(slot)
    arrive(0, 2)
    arrive(1, 2)
    for slot in (R3, L3):
        tile(slot, 0)
        tile(slot, 1)
        stats(slot)
    hops[0, 0, 3].wait_recv()
    hops[1, 1, 3].wait_recv()
    tile(FAR, 0)
    tile(FAR, 1)
    stats(FAR)

    order = (OWN, R1, L1, R2, L2, R3, L3, FAR)
    parts = []
    for slot in order:
        if slot == OWN:
            parts.append((part_tx[OWN, 0:2, :], part_tx[OWN, 2:4, :]))
        else:
            pltpu.make_async_remote_copy(
                src_ref=part_tx.at[slot], dst_ref=part_rx.at[slot],
                send_sem=st_send.at[slot], recv_sem=st_recv.at[slot],
                device_id=on_ring(PLACE[slot]), device_id_type=MESH,
            ).wait_recv()
            parts.append((part_rx[slot, 0:2, :], part_rx[slot, 2:4, :]))
    peak = parts[0][0]
    for log_part, _ in parts[1:]:
        peak = jnp.maximum(peak, log_part)
    total = jnp.zeros_like(peak)
    weighted = jnp.zeros_like(peak)
    for log_part, delta_part in parts:
        share = jnp.exp(log_part - peak)
        total = total + share
        weighted = weighted + share * delta_part
    fin[OWN, 0:2, :] = peak + jnp.log(total)
    fin[OWN, 2:4, :] = weighted / total
    fin_copies = {}
    for slot in (FAR, R3, L3, R2, L2, R1, L1):
        at = MIRROR[slot]
        fin_copies[at] = send(
            fin.at[OWN], fin.at[at], fin_send.at[slot], fin_recv.at[at], on_ring(PLACE[slot])
        )

    first = [True]

    def grads(slot):
        if slot != OWN:
            fin_copies[slot].wait_recv()
        log_total = jnp.concatenate([fin[slot, 0:1, :], fin[slot, 1:2, :]], axis=1)
        delta = jnp.concatenate([fin[slot, 2:3, :], fin[slot, 3:4, :]], axis=1)
        dq_t = None
        for kh in range(2):
            keys = pl.ds(kh * HALF, HALF)
            c = jnp.exp(mbuf[slot, kh, 0:1, :] - log_total)
            p = ebuf[slot, keys, :] * c
            prob_half = p.astype(BF16)
            score_grad = (p * (dbuf[slot, keys, :] - delta)).astype(BF16)
            dv = jnp.dot(prob_half, gbuf[slot], preferred_element_type=F32)
            dk = jnp.dot(score_grad, qbuf[slot], preferred_element_type=F32)
            if first[0]:
                dv_acc[keys, :] = dv
                dk_acc[keys, :] = dk
            else:
                dv_acc[keys, :] += dv
                dk_acc[keys, :] += dk
            t = jnp.dot(ktbuf[:, keys], score_grad, preferred_element_type=F32)
            dq_t = t if dq_t is None else dq_t + t
        first[0] = False
        return dq_t

    dq = {}

    def pass_sum(d, i, rows):
        n = d * 4 + i
        dq[d, i] = send(
            dq_tx.at[n, rows], dq_rx.at[n, rows], dq_send.at[n], dq_recv.at[n], (left, right)[d]
        )

    halves = (pl.ds(0, 64), pl.ds(64, 64))
    t = grads(FAR)
    dq_tx[0, 0:64, :] = t[0:64].astype(BF16)
    pass_sum(0, 0, halves[0])
    dq_tx[4, 64:128, :] = t[64:128].astype(BF16)
    pass_sum(1, 0, halves[1])
    for i, pair in enumerate(((R3, L3), (R2, L2), (R1, L1))):
        for d in (0, 1):
            t = grads(pair[d])
            dq[d, i].wait_recv()
            n = d * 4 + i
            if i == 0:
                dqt[...] = t
                dqt[halves[d], :] += dq_rx[n, halves[d], :].astype(F32)
                t = dqt[...]
            else:
                t = t + dq_rx[n].astype(F32)
            dq_tx[n + 1] = t.astype(BF16)
            pass_sum(d, i + 1, pl.ds(0, 128))
    dqt[...] = grads(OWN)

    red = []
    for j, p in enumerate((3, 1)):
        pair_tx[j, 0] = dk_acc[key_rows_at(p), :].astype(BF16)
        pair_tx[j, 1] = dv_acc[key_rows_at(p), :].astype(BF16)
        red.append(send(pair_tx.at[j], pair_rx.at[j], red_send.at[j], red_recv.at[j], sibling))
    red[0].wait_recv()
    far_tx[0] = (dk_acc[key_rows_at(2), :] + pair_rx[0, 0].astype(F32)).astype(BF16)
    far_tx[1] = (dv_acc[key_rows_at(2), :] + pair_rx[0, 1].astype(F32)).astype(BF16)
    red.append(send(far_tx, far_rx, red_send.at[2], red_recv.at[2], across))

    dq[0, 3].wait_recv()
    dq[1, 3].wait_recv()
    t = dqt[...] + dq_rx[3].astype(F32) + dq_rx[7].astype(F32)
    out_buf[0] = t.T * SCALE
    outs = [pltpu.make_async_copy(out_buf.at[0], dq_hbm, out_sem.at[0])]
    outs[0].start()
    red[1].wait_recv()
    red[2].wait_recv()
    for i, (acc, out, scale) in enumerate(((dk_acc, dk_hbm, SCALE), (dv_acc, dv_hbm, None))):
        t = acc[key_rows_at(0), :] + pair_rx[1, i].astype(F32) + far_rx[i].astype(F32)
        out_buf[1 + i] = t if scale is None else t * scale
        c = pltpu.make_async_copy(out_buf.at[1 + i], out, out_sem.at[1 + i])
        c.start()
        outs.append(c)
    for c in pending:
        c.wait_send()
    for c in outs:
        c.wait()


def shards(queries, key_rows, value_rows, out_grad):
    any_spec = pl.BlockSpec(memory_space=pl.ANY)
    dma = pltpu.SemaphoreType.DMA
    out = jax.ShapeDtypeStruct((ROWS, WIDTH), F32)
    vm = pltpu.VMEM
    return pl.pallas_call(
        kernel,
        out_shape=(out, out, out),
        in_specs=[any_spec] * 4,
        out_specs=(any_spec,) * 3,
        scratch_shapes=[
            vm((8, ROWS, WIDTH), BF16),
            vm((8, ROWS, WIDTH), BF16),
            vm((KEYS, WIDTH), BF16),
            vm((KEYS, WIDTH), BF16),
            vm((WIDTH, KEYS), BF16),
            vm((8, KEYS, ROWS), F32),
            vm((8, KEYS, ROWS), F32),
            vm((8, 2, 8, ROWS), F32),
            vm((8, 4, 128), F32),
            vm((8, 4, 128), F32),
            vm((8, 4, 128), F32),
            vm((KEYS, WIDTH), F32),
            vm((KEYS, WIDTH), F32),
            vm((WIDTH, ROWS), F32),
            vm((8, WIDTH, ROWS), BF16),
            vm((8, WIDTH, ROWS), BF16),
            vm((2, 2, ROWS, WIDTH), BF16),
            vm((2, 2, ROWS, WIDTH), BF16),
            vm((2, ROWS, WIDTH), BF16),
            vm((2, ROWS, WIDTH), BF16),
            vm((3, ROWS, WIDTH), F32),
            dma((4,)),
            dma((16,)),
            dma((16,)),
            dma((6,)),
            dma((6,)),
            dma((8,)),
            dma((8,)),
            dma((8,)),
            dma((8,)),
            dma((8,)),
            dma((8,)),
            dma((3,)),
            dma((3,)),
            dma((3,)),
        ],
        compiler_params=pltpu.CompilerParams(
            collective_id=0, has_side_effects=True, vmem_limit_bytes=56 * 1024 * 1024
        ),
        cost_estimate=pl.CostEstimate(
            flops=2 * 5 * KEYS * 8 * ROWS * WIDTH,
            bytes_accessed=4 * ROWS * WIDTH * 2 + 3 * ROWS * WIDTH * 4,
            transcendentals=KEYS * 8 * ROWS,
        ),
    )(queries, key_rows, value_rows, out_grad)


def solution(mesh):
    spec = P(("dp", "ctx"), None)
    return jax.shard_map(
        shards, mesh=mesh, in_specs=(spec,) * 4, out_specs=(spec,) * 3, check_vma=False
    )
```

time: 247 us -> 59.9 us (0.24)
  waiting for transfers between devices: 127 us -> 0 us
  matrix products: 61.7 us -> 0 us
  Pallas kernels: 0 us -> 55.9 us
  local copies, waits for them, and re-layouts: 20.5 us -> 3.21 us
  starting transfers between devices: 14.6 us -> 0 us
  between operations: 14.2 us -> 0.65 us
  other arithmetic: 6.49 us -> 0 us
    all_gather x2 -> x0, waiting for transfers between devices: 127 us -> none  [side_by_side(): whole = lax.all_gather(both, axis, axis=dim, tiled=True)]
    dot_general x56 -> x0, matrix products: 61.7 us -> none  [the longest x32 25.2 us: dot_rows(): lax.dot_general(left, right, (((1,), (1,)), ((), ())), preferred_element_...]
    pallas_call x0 -> x1, Pallas kernels: none -> 55.9 us  [shards(): pl.pallas_call(kernel, out_shape=(out, out, out), in_specs=[any_spec] * 4...]
    all_to_all x2 -> x0, starting transfers between devices: 14.5 us -> none  [copy_for_each(): lax.all_to_all(jnp.broadcast_to(shard[None], (size, *shard.shape)), axis,...]
    dynamic_slice x16 -> x0, local copies, waits for them, and re-layouts: 10.9 us -> none  [the longest x8 5.46 us: key_step(): log_part = lax.dynamic_slice_in_dim(all_log, offset, length, 0)]
    split x2 -> x0, local copies, waits for them, and re-layouts: 7.7 us -> none  [side_by_side(): jnp.split(whole, [sum(widths[:k]) for k in range(1, len(widths))], axis=a...]
    concatenate x2 -> x0, other arithmetic: 3.09 us -> none  [side_by_side(): both = jnp.concatenate(arrays, axis=along)]
    unnamed x10 -> x7, local copies, waits for them, and re-layouts: 0.58 us -> 3.21 us
  transfers between devices with their start and end apart: 4 -> 0, of which waited for: 2 -> 0; matrix products, arithmetic and copies ran while one was open for 17% -> 0% of each run, Pallas kernels for 0% -> 0%
where the time goes in v1:
time: 59.9 us; the launch traced here: 59.7 us
  Pallas kernels  55.9 us (93%)
  local copies, waits for them, and re-layouts  3.21 us (5%)
  between operations  0.65 us (1%)
    pallas_call x1, Pallas kernels, shards(): pl.pallas_call(kernel, out_shape=(out, out, out), in_specs=[any_spec] * 4...  55.9 us
    unnamed x7, local copies, waits for them, and re-layouts  3.21 us

profile of v1, /device:TPU:1, one launch (start us, length us, event | category | flops | bytes accessed | tf_op | source)
XLA Modules:
  0.0 59.7 jit_solution(8225057608028648362)
XLA Ops:
  0.6 55.9 %shard_map.67 = (f32[256,128]{1,0:T(8,128)}, f32[256,128]{1,0:T(8,128)}, f32[256,128]{1,0:T(8,128)}) custom-call(bf16[256,128]{1,0:T(8,128)(2,1)} %q_hbm.1, bf16[256,128]{1,0:T(8,128)(2,1)} %k_hbm.1, bf16[256,128]{1,0:T(8,128)(2,1)} %v_hbm.1, bf16[256,128]{1,0:T(8,128)(2,1)} %g_hbm.1), custom_call_target="tpu_custom_call" | custom-call | flops 2684354560 | bytes 655360 | tf_op jit(solution)/shard_map/pallas_call | solution.py:323
  56.5 0.0 copy-start.1
  56.5 1.6 %copy.10 = f32[256,128]{1,0:T(8,128)} copy(f32[256,128]{1,0:T(8,128)} %get-tuple-element.6) | data formatting | bytes 262144
  58.1 0.0 copy-done.1
  58.1 0.0 copy-start
  58.1 0.7 %copy.11 = f32[256,128]{1,0:T(8,128)} copy(f32[256,128]{1,0:T(8,128)S(1)} %copy-done.1) | data formatting | bytes 262144
  58.8 0.3 copy-done
  59.1 0.7 %copy.12 = f32[256,128]{1,0:T(8,128)} copy(f32[256,128]{1,0:T(8,128)S(1)} %copy-done) | data formatting | bytes 262144
Async XLA Ops:
  56.5 1.6 %copy-start.1 = (f32[256,128]{1,0:T(8,128)S(1)}, f32[256,128]{1,0:T(8,128)}, u32[]{:S(2)}) copy-start(f32[256,128]{1,0:T(8,128)} %get-tuple-element.7) | copy-start | bytes 393220
  58.1 1.0 %copy-start = (f32[256,128]{1,0:T(8,128)S(1)}, f32[256,128]{1,0:T(8,128)}, u32[]{:S(2)}) copy-start(f32[256,128]{1,0:T(8,128)} %get-tuple-element.8) | copy-start | bytes 393220

commit v2 on v1

--- a/solution.py
+++ b/solution.py
@@ -19,9 +19,11 @@
 SCALE = WIDTH ** (-0.5)
 EXP2_SCALE = SCALE * math.log2(math.e)
 
-OWN, FAR, R1, L1, R2, L2, R3, L3 = range(8)
-PLACE = (0, 4, -1, 1, -2, 2, -3, 3)
-MIRROR = (OWN, FAR, L1, R1, L2, R2, L3, R3)
+OWN, R1, L1, R2, L2, R3, L3, FAR = range(8)
+PLACE = (0, -1, 1, -2, 2, -3, 3, 4)
+SLOT_AT = {p % RING: s for s, p in enumerate(PLACE)}
+MIRROR = tuple(SLOT_AT[-p % RING] for p in PLACE)
+PIECE = 128
 
 
 def rows_dot(left, right):
@@ -32,9 +34,9 @@
     q_hbm, k_hbm, v_hbm, g_hbm,
     dq_hbm, dk_hbm, dv_hbm,
     qbuf, gbuf, kbuf, vbuf, ktbuf, ebuf, dbuf, mbuf,
-    part_tx, part_rx, fin, dk_acc, dv_acc,
+    part_tx, part_rx, dk_acc, dv_acc,
     dqt, dq_tx, dq_rx, pair_tx, pair_rx, far_tx, far_rx, out_buf,
-    in_sem, gat_send, gat_recv, kv_send, kv_recv, st_send, st_recv, fin_send, fin_recv,
+    in_sem, gat_send, gat_recv, kv_send, kv_recv, st_send, st_recv,
     dq_send, dq_recv, red_send, red_recv, out_sem,
 ):
     me = lax.axis_index("ctx")
@@ -48,9 +50,10 @@
 
     sibling = {"ctx": z * 4 + xh * 2 + (1 - core)}
     across = {"ctx": z * 4 + (1 - xh) * 2 + core}
+    right, left = on_ring(1), on_ring(-1)
 
     barrier = pltpu.get_barrier_semaphore()
-    for peer in [on_ring(PLACE[s]) for s in range(1, 8)] + [sibling, across]:
+    for peer in (right, left, across, sibling):
         pl.semaphore_signal(barrier, inc=1, device_id=peer, device_id_type=MESH)
 
     own_rows = pl.ds(0, ROWS)
@@ -80,17 +83,15 @@
 
     for c in loads:
         c.wait()
-    pl.semaphore_wait(barrier, 9)
-
-    right, left = on_ring(1), on_ring(-1)
-
-    bufs = (qbuf, gbuf)
+    pl.semaphore_wait(barrier, 4)
 
     def hop(b, d, i):
         slots = ((OWN, R1, R2, R3, FAR), (OWN, L1, L2, L3, FAR))[d]
         n = (b * 2 + d) * 4 + i
+        buf = (qbuf, gbuf)[b // 2]
+        rows = pl.ds((b % 2) * PIECE, PIECE)
         return send(
-            bufs[b].at[slots[i]], bufs[b].at[slots[i + 1]],
+            buf.at[slots[i], rows], buf.at[slots[i + 1], rows],
             gat_send.at[n], gat_recv.at[n], (right, left)[d],
         )
 
@@ -98,7 +99,7 @@
         return pl.ds(p * ROWS, ROWS)
 
     hops = {}
-    for b in (0, 1):
+    for b in range(4):
         for d in (0, 1):
             hops[b, d, 0] = hop(b, d, 0)
     kv_across = []
@@ -132,110 +133,121 @@
         mbuf[slot, kh, 1:2, :] = jnp.sum(e, axis=0, keepdims=True)
         mbuf[slot, kh, 2:3, :] = jnp.sum(e * d, axis=0, keepdims=True)
 
-    def put_stats(ref, log_total, delta):
-        for i in range(2):
-            cols = slice(i * 128, (i + 1) * 128)
-            ref[i : i + 1, :] = log_total[:, cols]
-            ref[2 + i : 3 + i, :] = delta[:, cols]
-
-    st = {}
-
     def stats(slot):
         m0, l0, w0 = (mbuf[slot, 0, i : i + 1, :] for i in range(3))
         m1, l1, w1 = (mbuf[slot, 1, i : i + 1, :] for i in range(3))
         m = jnp.maximum(m0, m1)
         a0, a1 = jnp.exp(m0 - m), jnp.exp(m1 - m)
         total = l0 * a0 + l1 * a1
-        put_stats(part_tx.at[slot], m + jnp.log(total), (w0 * a0 + w1 * a1) / total)
-        if slot != OWN:
+        log_total = m + jnp.log(total)
+        delta = (w0 * a0 + w1 * a1) / total
+        for i in range(2):
+            cols = slice(i * 128, (i + 1) * 128)
+            part_tx[slot, i : i + 1, :] = log_total[:, cols]
+            part_tx[slot, 2 + i : 3 + i, :] = delta[:, cols]
+
+    groups = (pl.ds(0, 5), pl.ds(5, 2), pl.ds(7, 1))
+    st = {}
+
+    def share_stats(g):
+        for slot in (FAR, R3, L3, R2, L2, R1, L1):
             at = MIRROR[slot]
-            st[slot] = send(
-                part_tx.at[slot], part_rx.at[at], st_send.at[slot], st_recv.at[at], on_ring(PLACE[slot])
+            st[at, g] = send(
+                part_tx.at[groups[g]], part_rx.at[at, groups[g]],
+                st_send.at[slot, g], st_recv.at[at, g], on_ring(PLACE[slot]),
             )
-
-    def wait_gather(b, i):
-        hops[b, 0, i].wait_recv()
-        if i < 3 or b == 0:
-            pass
 
     def arrive(b, i):
         for d in (0, 1):
             hops[b, d, i].wait_recv()
-            if i < 2 or b == d:
+            if i < 2 or b // 2 == d:
                 hops[b, d, i + 1] = hop(b, d, i + 1)
 
     for c in kv_sibling:
         c.wait_recv()
     tile(OWN, 0)
-    arrive(0, 0)
-    arrive(1, 0)
+    for b in range(4):
+        arrive(b, 0)
     tile(R1, 0)
+    pass_keys_on()
     tile(L1, 0)
-    pass_keys_on()
     arrive(0, 1)
     for c in kv_third:
         c.wait_recv()
-    for p in range(4):
-        ktbuf[:, p * ROWS : (p + 1) * ROWS] = kbuf[key_rows_at(p), :].astype(F32).T.astype(BF16)
     tile(OWN, 1)
-    stats(OWN)
     arrive(1, 1)
-    for slot in (R1, L1):
-        tile(slot, 1)
+    tile(R1, 1)
+    arrive(2, 1)
+    tile(L1, 1)
+    arrive(3, 1)
+    for slot in (OWN, R1, L1):
         stats(slot)
-    for slot in (R2, L2):
-        tile(slot, 0)
-        tile(slot, 1)
-        stats(slot)
+    tile(R2, 0)
+    tile(R2, 1)
     arrive(0, 2)
     arrive(1, 2)
+    tile(L2, 0)
+    arrive(2, 2)
+    tile(L2, 1)
+    arrive(3, 2)
+    stats(R2)
+    stats(L2)
+    share_stats(0)
     for slot in (R3, L3):
         tile(slot, 0)
         tile(slot, 1)
         stats(slot)
-    hops[0, 0, 3].wait_recv()
-    hops[1, 1, 3].wait_recv()
+    share_stats(1)
+    for p in range(4):
+        ktbuf[:, p * ROWS : (p + 1) * ROWS] = kbuf[key_rows_at(p), :].astype(F32).T.astype(BF16)
+    for b in range(4):
+        hops[b, b // 2, 3].wait_recv()
     tile(FAR, 0)
     tile(FAR, 1)
     stats(FAR)
-
-    order = (OWN, R1, L1, R2, L2, R3, L3, FAR)
-    parts = []
-    for slot in order:
-        if slot == OWN:
-            parts.append((part_tx[OWN, 0:2, :], part_tx[OWN, 2:4, :]))
-        else:
-            pltpu.make_async_remote_copy(
-                src_ref=part_tx.at[slot], dst_ref=part_rx.at[slot],
-                send_sem=st_send.at[slot], recv_sem=st_recv.at[slot],
-                device_id=on_ring(PLACE[slot]), device_id_type=MESH,
-            ).wait_recv()
-            parts.append((part_rx[slot, 0:2, :], part_rx[slot, 2:4, :]))
-    peak = parts[0][0]
-    for log_part, _ in parts[1:]:
-        peak = jnp.maximum(peak, log_part)
-    total = jnp.zeros_like(peak)
-    weighted = jnp.zeros_like(peak)
-    for log_part, delta_part in parts:
-        share = jnp.exp(log_part - peak)
-        total = total + share
-        weighted = weighted + share * delta_part
-    fin[OWN, 0:2, :] = peak + jnp.log(total)
-    fin[OWN, 2:4, :] = weighted / total
-    fin_copies = {}
-    for slot in (FAR, R3, L3, R2, L2, R1, L1):
-        at = MIRROR[slot]
-        fin_copies[at] = send(
-            fin.at[OWN], fin.at[at], fin_send.at[slot], fin_recv.at[at], on_ring(PLACE[slot])
-        )
+    share_stats(2)
+
+    order = (FAR, R3, L3, R2, L2, R1, L1, OWN)
+    for g in range(2):
+        for u in range(1, 8):
+            st[u, g].wait_recv()
+    partial = {}
+
+    def parts_of(t, u):
+        s = SLOT_AT[(PLACE[t] - PLACE[u]) % RING]
+        ref = part_tx if u == OWN else part_rx.at[u]
+        return s, ref
+
+    def combine(parts):
+        peak = parts[0][0]
+        for part in parts[1:]:
+            peak = jnp.maximum(peak, part[0])
+        total = jnp.zeros_like(peak)
+        weighted = jnp.zeros_like(peak)
+        for log_part, delta_part in parts:
+            share = jnp.exp(log_part - peak)
+            total = total + share
+            weighted = weighted + share * delta_part
+        return peak + jnp.log(total), weighted / total
+
+    for t in order:
+        early = []
+        for u in range(8):
+            s, ref = parts_of(t, u)
+            if s != FAR:
+                early.append((ref[s, 0:2, :], ref[s, 2:4, :]))
+        partial[t] = combine(early)
+    for u in range(1, 8):
+        st[u, 2].wait_recv()
 
     first = [True]
 
     def grads(slot):
-        if slot != OWN:
-            fin_copies[slot].wait_recv()
-        log_total = jnp.concatenate([fin[slot, 0:1, :], fin[slot, 1:2, :]], axis=1)
-        delta = jnp.concatenate([fin[slot, 2:3, :], fin[slot, 3:4, :]], axis=1)
+        u = SLOT_AT[(PLACE[slot] - 4) % RING]
+        s, ref = parts_of(slot, u)
+        log_total, delta = combine([partial[slot], (ref[s, 0:2, :], ref[s, 2:4, :])])
+        log_total = jnp.concatenate([log_total[0:1], log_total[1:2]], axis=1)
+        delta = jnp.concatenate([delta[0:1], delta[1:2]], axis=1)
         dq_t = None
         for kh in range(2):
             keys = pl.ds(kh * HALF, HALF)
@@ -257,47 +269,51 @@
         return dq_t
 
     dq = {}
-
-    def pass_sum(d, i, rows):
-        n = d * 4 + i
-        dq[d, i] = send(
-            dq_tx.at[n, rows], dq_rx.at[n, rows], dq_send.at[n], dq_recv.at[n], (left, right)[d]
-        )
-
-    halves = (pl.ds(0, 64), pl.ds(64, 64))
+    whole = pl.ds(0, WIDTH)
+    far_rows = (pl.ds(0, 64), pl.ds(64, 64))
+
+    def send_sum(d, kind, value):
+        n = d * 4 + kind
+        rows = far_rows[d] if kind == 0 else whole
+        dq_tx[n, rows, :] = value.astype(BF16)
+        steps = (2, 1, 2, 1)[kind]
+        dq[d, kind] = send(
+            dq_tx.at[n, rows], dq_rx.at[n, rows], dq_send.at[n], dq_recv.at[n],
+            on_ring(steps if d else -steps),
+        )
+
     t = grads(FAR)
-    dq_tx[0, 0:64, :] = t[0:64].astype(BF16)
-    pass_sum(0, 0, halves[0])
-    dq_tx[4, 64:128, :] = t[64:128].astype(BF16)
-    pass_sum(1, 0, halves[1])
-    for i, pair in enumerate(((R3, L3), (R2, L2), (R1, L1))):
-        for d in (0, 1):
-            t = grads(pair[d])
-            dq[d, i].wait_recv()
-            n = d * 4 + i
-            if i == 0:
-                dqt[...] = t
-                dqt[halves[d], :] += dq_rx[n, halves[d], :].astype(F32)
-                t = dqt[...]
-            else:
-                t = t + dq_rx[n].astype(F32)
-            dq_tx[n + 1] = t.astype(BF16)
-            pass_sum(d, i + 1, pl.ds(0, 128))
-    dqt[...] = grads(OWN)
+    send_sum(0, 0, t[0:64])
+    send_sum(1, 0, t[64:128])
+    send_sum(0, 1, grads(R3))
+    send_sum(1, 1, grads(L3))
+    dqt[0] = grads(R2)
+    dqt[1] = grads(L2)
+    send_sum(0, 3, grads(R1))
+    send_sum(1, 3, grads(L1))
+    dqt[2] = grads(OWN)
 
     red = []
     for j, p in enumerate((3, 1)):
         pair_tx[j, 0] = dk_acc[key_rows_at(p), :].astype(BF16)
         pair_tx[j, 1] = dv_acc[key_rows_at(p), :].astype(BF16)
         red.append(send(pair_tx.at[j], pair_rx.at[j], red_send.at[j], red_recv.at[j], sibling))
+    for d in (0, 1):
+        dq[d, 0].wait_recv()
+        dq[d, 1].wait_recv()
+        dqt[d, far_rows[d], :] += dq_rx[d * 4, far_rows[d], :].astype(F32)
+        send_sum(d, 2, dqt[d] + dq_rx[d * 4 + 1].astype(F32))
     red[0].wait_recv()
     far_tx[0] = (dk_acc[key_rows_at(2), :] + pair_rx[0, 0].astype(F32)).astype(BF16)
     far_tx[1] = (dv_acc[key_rows_at(2), :] + pair_rx[0, 1].astype(F32)).astype(BF16)
     red.append(send(far_tx, far_rx, red_send.at[2], red_recv.at[2], across))
 
-    dq[0, 3].wait_recv()
-    dq[1, 3].wait_recv()
-    t = dqt[...] + dq_rx[3].astype(F32) + dq_rx[7].astype(F32)
+    for d in (0, 1):
+        dq[d, 3].wait_recv()
+    t = dqt[2] + dq_rx[3].astype(F32) + dq_rx[7].astype(F32)
+    for d in (0, 1):
+        dq[d, 2].wait_recv()
+    t = t + dq_rx[2].astype(F32) + dq_rx[6].astype(F32)
     out_buf[0] = t.T * SCALE
     outs = [pltpu.make_async_copy(out_buf.at[0], dq_hbm, out_sem.at[0])]
     outs[0].start()
@@ -335,11 +351,10 @@
             vm((8, KEYS, ROWS), F32),
             vm((8, 2, 8, ROWS), F32),
             vm((8, 4, 128), F32),
-            vm((8, 4, 128), F32),
-            vm((8, 4, 128), F32),
+            vm((8, 8, 4, 128), F32),
             vm((KEYS, WIDTH), F32),
             vm((KEYS, WIDTH), F32),
-            vm((WIDTH, ROWS), F32),
+            vm((3, WIDTH, ROWS), F32),
             vm((8, WIDTH, ROWS), BF16),
             vm((8, WIDTH, ROWS), BF16),
             vm((2, 2, ROWS, WIDTH), BF16),
@@ -348,14 +363,12 @@
             vm((2, ROWS, WIDTH), BF16),
             vm((3, ROWS, WIDTH), F32),
             dma((4,)),
-            dma((16,)),
-            dma((16,)),
+            dma((32,)),
+            dma((32,)),
             dma((6,)),
             dma((6,)),
-            dma((8,)),
-            dma((8,)),
-            dma((8,)),
-            dma((8,)),
+            dma((8, 3)),
+            dma((8, 3)),
             dma((8,)),
             dma((8,)),
             dma((3,)),

time: 59.9 us -> 46.7 us (0.78)
  the two profiles are of different devices: /device:TPU:1 before, /device:TPU:16 now
where the time goes in v2:
time: 46.7 us; the launch traced here: 46.6 us
  Pallas kernels  42.7 us (91%)
  local copies, waits for them, and re-layouts  3.21 us (7%)
  between operations  0.65 us (1%)
    pallas_call x1, Pallas kernels, shards(): pl.pallas_call(kernel, out_shape=(out, out, out), in_specs=[any_spec] * 4...  42.7 us
    unnamed x7, local copies, waits for them, and re-layouts  3.21 us

profile of v2, /device:TPU:16, one launch (start us, length us, event | category | flops | bytes accessed | tf_op | source)
XLA Modules:
  0.0 46.6 jit_solution(2775664316391573521)
XLA Ops:
  0.6 42.7 %shard_map.67 = (f32[256,128]{1,0:T(8,128)}, f32[256,128]{1,0:T(8,128)}, f32[256,128]{1,0:T(8,128)}) custom-call(bf16[256,128]{1,0:T(8,128)(2,1)} %q_hbm.1, bf16[256,128]{1,0:T(8,128)(2,1)} %k_hbm.1, bf16[256,128]{1,0:T(8,128)(2,1)} %v_hbm.1, bf16[256,128]{1,0:T(8,128)(2,1)} %g_hbm.1), custom_call_target="tpu_custom_call" | custom-call | flops 2684354560 | bytes 655360 | tf_op jit(solution)/shard_map/pallas_call | solution.py:339
  43.4 0.0 copy-start.1
  43.4 1.6 %copy.10 = f32[256,128]{1,0:T(8,128)} copy(f32[256,128]{1,0:T(8,128)} %get-tuple-element.6) | data formatting | bytes 262144
  45.0 0.0 copy-done.1
  45.0 0.0 copy-start
  45.0 0.7 %copy.11 = f32[256,128]{1,0:T(8,128)} copy(f32[256,128]{1,0:T(8,128)S(1)} %copy-done.1) | data formatting | bytes 262144
  45.6 0.3 copy-done
  45.9 0.7 %copy.12 = f32[256,128]{1,0:T(8,128)} copy(f32[256,128]{1,0:T(8,128)S(1)} %copy-done) | data formatting | bytes 262144
Async XLA Ops:
  43.4 1.6 %copy-start.1 = (f32[256,128]{1,0:T(8,128)S(1)}, f32[256,128]{1,0:T(8,128)}, u32[]{:S(2)}) copy-start(f32[256,128]{1,0:T(8,128)} %get-tuple-element.7) | copy-start | bytes 393220
  45.0 1.0 %copy-start = (f32[256,128]{1,0:T(8,128)S(1)}, f32[256,128]{1,0:T(8,128)}, u32[]{:S(2)}) copy-start(f32[256,128]{1,0:T(8,128)} %get-tuple-element.8) | copy-start | bytes 393220

commit v3 on v2

v3 whole, which is shorter than its diff:
```python
import math

import jax
import jax.numpy as jnp
from jax import lax
from jax.experimental import pallas as pl
from jax.experimental.pallas import tpu as pltpu
from jax.sharding import PartitionSpec as P

F32 = jnp.float32
BF16 = jnp.bfloat16
MESH = pl.DeviceIdType.MESH

ROWS = 256
WIDTH = 128
RING = 8
HALF = 512
KEYS = 1024
SCALE = WIDTH ** (-0.5)
EXP2_SCALE = SCALE * math.log2(math.e)

OWN, R1, L1, R2, L2, R3, L3, FAR = range(8)
PLACE = (0, -1, 1, -2, 2, -3, 3, 4)
SLOT_AT = {p % RING: s for s, p in enumerate(PLACE)}
MIRROR = tuple(SLOT_AT[-p % RING] for p in PLACE)
PIECE = 128

Q_PATH = ((OWN, R1, 1), (OWN, L1, -1), (R1, R2, 1), (L1, L2, -1), (R2, FAR, 2), (R2, R3, 1), (L2, L3, -1))
G_PATH = ((OWN, R1, 1), (OWN, L1, -1), (R1, R2, 1), (L1, L2, -1), (L2, FAR, -2), (R2, R3, 1), (L2, L3, -1))
PIECES = ((0, 2), (1, 3), (2, 0), (3, 1))


def rows_dot(left, right):
    return lax.dot_general(left, right, (((1,), (1,)), ((), ())), preferred_element_type=F32)


def kernel(
    q_hbm, k_hbm, v_hbm, g_hbm,
    dq_out, dk_out, dv_out,
    qbuf, gbuf, kbuf, vbuf, ktbuf, ebuf, dbuf, mbuf,
    part_tx, part_rx, dk_acc, dv_acc,
    dqt, dq_tx, dq_rx, pair_tx, pair_rx, far_tx, far_rx,
    in_sem, gat_send, gat_recv, kv_send, kv_recv, st_send, st_recv,
    dq_send, dq_recv, red_send, red_recv,
):
    me = lax.axis_index("ctx")
    z = me // 4
    w = me % 4
    core = w % 2
    xh = w // 2

    def on_ring(offset):
        return {"ctx": ((z + (offset + RING)) % RING) * 4 + w}

    sibling = {"ctx": z * 4 + xh * 2 + (1 - core)}
    across = {"ctx": z * 4 + (1 - xh) * 2 + core}
    right, left = on_ring(1), on_ring(-1)

    barrier = pltpu.get_barrier_semaphore()
    for peer in (right, left, across, sibling):
        pl.semaphore_signal(barrier, inc=1, device_id=peer, device_id_type=MESH)

    own_rows = pl.ds(0, ROWS)
    loads = [
        pltpu.make_async_copy(src, dst, in_sem.at[i])
        for i, (src, dst) in enumerate(
            (
                (q_hbm, qbuf.at[OWN]),
                (g_hbm, gbuf.at[OWN]),
                (k_hbm, kbuf.at[own_rows]),
                (v_hbm, vbuf.at[own_rows]),
            )
        )
    ]
    for c in loads:
        c.start()
    pending = []

    def send(src, dst, send_sem, recv_sem, peer):
        c = pltpu.make_async_remote_copy(
            src_ref=src, dst_ref=dst, send_sem=send_sem, recv_sem=recv_sem,
            device_id=peer, device_id_type=MESH,
        )
        c.start()
        pending.append(c)
        return c

    for c in loads:
        c.wait()
    pl.semaphore_wait(barrier, 4)

    hops = {}

    def pass_on(piece, slot, way=None):
        buf, path = ((qbuf, Q_PATH), (gbuf, G_PATH))[piece // 2]
        rows = pl.ds((piece % 2) * PIECE, PIECE)
        for src, dst, steps in path:
            if src == slot and way in (None, steps > 0):
                n = piece * 8 + dst
                hops[piece, dst] = send(
                    buf.at[src, rows], buf.at[dst, rows], gat_send.at[n], gat_recv.at[n], on_ring(steps)
                )

    def arrive(piece, slot):
        hops[piece, slot].wait_recv()
        pass_on(piece, slot)

    def key_rows_at(p):
        return pl.ds(p * ROWS, ROWS)

    for a, b in PIECES:
        pass_on(a, OWN, True)
        pass_on(b, OWN, False)
    kv_across = []
    for i, buf in enumerate((kbuf, vbuf)):
        kv_across.append(
            send(buf.at[key_rows_at(0)], buf.at[key_rows_at(2)], kv_send.at[i], kv_recv.at[i], across)
        )
    kv_sibling = []
    for i, buf in enumerate((kbuf, vbuf)):
        kv_sibling.append(
            send(buf.at[key_rows_at(0)], buf.at[key_rows_at(1)], kv_send.at[2 + i], kv_recv.at[2 + i], sibling)
        )
    kv_third = []

    def pass_keys_on():
        for i, buf in enumerate((kbuf, vbuf)):
            kv_across[i].wait_recv()
            kv_third.append(
                send(buf.at[key_rows_at(2)], buf.at[key_rows_at(3)], kv_send.at[4 + i], kv_recv.at[4 + i], sibling)
            )

    def tile(slot, kh):
        keys = pl.ds(kh * HALF, HALF)
        s = rows_dot(kbuf[keys, :], qbuf[slot])
        m = jnp.max(s, axis=0, keepdims=True)
        e = jnp.exp2((s - m) * EXP2_SCALE)
        ebuf[slot, keys, :] = e
        d = rows_dot(vbuf[keys, :], gbuf[slot])
        dbuf[slot, keys, :] = d
        mbuf[slot, kh, 0:1, :] = m * SCALE
        mbuf[slot, kh, 1:2, :] = jnp.sum(e, axis=0, keepdims=True)
        mbuf[slot, kh, 2:3, :] = jnp.sum(e * d, axis=0, keepdims=True)

    def stats(slot):
        m0, l0, w0 = (mbuf[slot, 0, i : i + 1, :] for i in range(3))
        m1, l1, w1 = (mbuf[slot, 1, i : i + 1, :] for i in range(3))
        m = jnp.maximum(m0, m1)
        a0, a1 = jnp.exp(m0 - m), jnp.exp(m1 - m)
        total = l0 * a0 + l1 * a1
        log_total = m + jnp.log(total)
        delta = (w0 * a0 + w1 * a1) / total
        for i in range(2):
            cols = slice(i * 128, (i + 1) * 128)
            part_tx[slot, i : i + 1, :] = log_total[:, cols]
            part_tx[slot, 2 + i : 3 + i, :] = delta[:, cols]

    groups = (pl.ds(0, 5), pl.ds(5, 2), pl.ds(7, 1))
    st = {}

    def share_stats(g):
        for slot in (FAR, R3, L3, R2, L2, R1, L1):
            at = MIRROR[slot]
            st[at, g] = send(
                part_tx.at[groups[g]], part_rx.at[at, groups[g]],
                st_send.at[slot, g], st_recv.at[at, g], on_ring(PLACE[slot]),
            )

    for c in kv_sibling:
        c.wait_recv()
    tile(OWN, 0)
    for a, b in PIECES:
        arrive(a, R1)
        arrive(b, L1)
    pass_keys_on()
    tile(R1, 0)
    tile(L1, 0)
    for a, b in PIECES[:2]:
        arrive(a, R2)
        arrive(b, L2)
    for c in kv_third:
        c.wait_recv()
    tile(OWN, 1)
    for a, b in PIECES[2:]:
        arrive(a, R2)
        arrive(b, L2)
    for slot in (R1, L1):
        tile(slot, 1)
    for slot in (OWN, R1, L1):
        stats(slot)
    for slot in (R2, L2):
        tile(slot, 0)
        tile(slot, 1)
        stats(slot)
    for p in range(4):
        ktbuf[:, p * ROWS : (p + 1) * ROWS] = kbuf[key_rows_at(p), :].astype(F32).T.astype(BF16)
    for slot in (R3, L3):
        for piece in range(4):
            arrive(piece, slot)
        if slot == R3:
            share_stats(0)
        tile(slot, 0)
        tile(slot, 1)
        stats(slot)
    share_stats(1)
    for piece in range(4):
        arrive(piece, FAR)
    tile(FAR, 0)
    tile(FAR, 1)
    stats(FAR)
    share_stats(2)

    order = (FAR, R3, L3, R2, L2, R1, L1, OWN)
    for g in range(2):
        for u in range(1, 8):
            st[u, g].wait_recv()
    partial = {}

    def parts_of(t, u):
        s = SLOT_AT[(PLACE[t] - PLACE[u]) % RING]
        ref = part_tx if u == OWN else part_rx.at[u]
        return s, ref

    def combine(parts):
        peak = parts[0][0]
        for part in parts[1:]:
            peak = jnp.maximum(peak, part[0])
        total = jnp.zeros_like(peak)
        weighted = jnp.zeros_like(peak)
        for log_part, delta_part in parts:
            share = jnp.exp(log_part - peak)
            total = total + share
            weighted = weighted + share * delta_part
        return peak + jnp.log(total), weighted / total

    for t in order:
        early = []
        for u in range(8):
            s, ref = parts_of(t, u)
            if s != FAR:
                early.append((ref[s, 0:2, :], ref[s, 2:4, :]))
        partial[t] = combine(early)
    for u in range(1, 8):
        st[u, 2].wait_recv()

    rows_stats = {}

    def grads(slot, kh):
        if slot not in rows_stats:
            u = SLOT_AT[(PLACE[slot] - 4) % RING]
            s, ref = parts_of(slot, u)
            log_total, delta = combine([partial[slot], (ref[s, 0:2, :], ref[s, 2:4, :])])
            rows_stats[slot] = tuple(
                jnp.concatenate([x[0:1], x[1:2]], axis=1) for x in (log_total, delta)
            )
        log_total, delta = rows_stats[slot]
        keys = pl.ds(kh * HALF, HALF)
        c = jnp.exp(mbuf[slot, kh, 0:1, :] - log_total)
        p = ebuf[slot, keys, :] * c
        prob_half = p.astype(BF16)
        score_grad = (p * (dbuf[slot, keys, :] - delta)).astype(BF16)
        dv = jnp.dot(prob_half, gbuf[slot], preferred_element_type=F32)
        dk = jnp.dot(score_grad, qbuf[slot], preferred_element_type=F32)
        if slot == R3:
            dv_acc[keys, :] = dv
            dk_acc[keys, :] = dk
        else:
            dv_acc[keys, :] += dv
            dk_acc[keys, :] += dk
        return jnp.dot(ktbuf[:, keys], score_grad, preferred_element_type=F32)

    dq = {}

    def send_sum(d, kind, h, value):
        n = (d * 4 + kind) * 2 + h
        dq_tx[n] = value.astype(BF16)
        steps = (4, 1, 2, 1)[kind]
        dq[d, kind, h] = send(
            dq_tx.at[n], dq_rx.at[n], dq_send.at[n], dq_recv.at[n], on_ring(steps if d else -steps)
        )

    def received(d, kind, h):
        dq[d, kind, h].wait_recv()
        return dq_rx[(d * 4 + kind) * 2 + h].astype(F32)

    wide = (slice(0, 64), slice(64, 128))
    for d, slot in enumerate((R3, L3)):
        t = grads(slot, 0) + grads(slot, 1)
        for h in (0, 1):
            send_sum(d, 1, h, t[wide[h]])
    t = grads(FAR, 0) + grads(FAR, 1)
    for h in (0, 1):
        send_sum(h, 0, h, t[wide[h]])
    for d, slot in enumerate((R2, L2)):
        dqt[slot] = grads(slot, 1) + grads(slot, 0)

    for slot in (R1, L1, OWN):
        dqt[slot] = grads(slot, 1)
    accs = (dk_acc, dv_acc)
    pair = {}
    across_sum = []

    def send_pair(j, p):
        for i, acc in enumerate(accs):
            n = j * 2 + i
            pair_tx[n] = acc[key_rows_at(p), :].astype(BF16)
            pair[j, i] = send(pair_tx.at[n], pair_rx.at[n], red_send.at[n], red_recv.at[n], sibling)

    def from_pair(j, i):
        pair[j, i].wait_recv()
        return pair_rx[j * 2 + i].astype(F32)

    send_pair(0, 3)
    for d, slot in enumerate((R1, L1)):
        t = dqt[slot] + grads(slot, 0)
        for h in (0, 1):
            send_sum(d, 3, h, t[wide[h]])
    dqt[OWN] += grads(OWN, 0)
    send_pair(1, 1)
    for i, acc in enumerate(accs):
        far_tx[i] = (acc[key_rows_at(2), :] + from_pair(0, i)).astype(BF16)
        across_sum.append(
            send(far_tx.at[i], far_rx.at[i], red_send.at[4 + i], red_recv.at[4 + i], across)
        )
    for d, slot in enumerate((R2, L2)):
        for h in (0, 1):
            send_sum(d, 2, h, dqt[slot, wide[h], :] + received(d, 1, h))

    for h in (0, 1):
        for d in (0, 1):
            dqt[OWN, wide[h], :] += received(d, 3, h)
    for h in (0, 1):
        dqt[OWN, wide[h], :] += received(h, 0, h)
    for i, (acc, out, scale) in enumerate(((dk_acc, dk_out, SCALE), (dv_acc, dv_out, None))):
        t = acc[key_rows_at(0), :] + from_pair(1, i)
        across_sum[i].wait_recv()
        t = t + far_rx[i].astype(F32)
        out[...] = t if scale is None else t * scale
    for h in (0, 1):
        for d in (0, 1):
            dqt[OWN, wide[h], :] += received(d, 2, h)
    dq_out[...] = dqt[OWN].T * SCALE
    for c in pending:
        c.wait_send()


def write_out(a_ref, b_ref, c_ref, a_out, b_out, c_out, sems):
    copies = [
        pltpu.make_async_copy(src, dst, sems.at[i])
        for i, (src, dst) in enumerate(((a_ref, a_out), (b_ref, b_out), (c_ref, c_out)))
    ]
    for c in copies:
        c.start()
    for c in copies:
        c.wait()


def shards(queries, key_rows, value_rows, out_grad):
    any_spec = pl.BlockSpec(memory_space=pl.ANY)
    dma = pltpu.SemaphoreType.DMA
    out = jax.ShapeDtypeStruct((ROWS, WIDTH), F32)
    near = pltpu.VMEM((ROWS, WIDTH), F32)
    near_spec = pl.BlockSpec(memory_space=pltpu.VMEM)
    vm = pltpu.VMEM
    grads = pl.pallas_call(
        kernel,
        out_shape=(near, near, near),
        in_specs=[any_spec] * 4,
        out_specs=(near_spec,) * 3,
        scratch_shapes=[
            vm((8, ROWS, WIDTH), BF16),
            vm((8, ROWS, WIDTH), BF16),
            vm((KEYS, WIDTH), BF16),
            vm((KEYS, WIDTH), BF16),
            vm((WIDTH, KEYS), BF16),
            vm((8, KEYS, ROWS), F32),
            vm((8, KEYS, ROWS), F32),
            vm((8, 2, 8, ROWS), F32),
            vm((8, 4, 128), F32),
            vm((8, 8, 4, 128), F32),
            vm((KEYS, WIDTH), F32),
            vm((KEYS, WIDTH), F32),
            vm((5, WIDTH, ROWS), F32),
            vm((16, WIDTH // 2, ROWS), BF16),
            vm((16, WIDTH // 2, ROWS), BF16),
            vm((4, ROWS, WIDTH), BF16),
            vm((4, ROWS, WIDTH), BF16),
            vm((2, ROWS, WIDTH), BF16),
            vm((2, ROWS, WIDTH), BF16),
            dma((4,)),
            dma((32,)),
            dma((32,)),
            dma((6,)),
            dma((6,)),
            dma((8, 3)),
            dma((8, 3)),
            dma((16,)),
            dma((16,)),
            dma((6,)),
            dma((6,)),
        ],
        compiler_params=pltpu.CompilerParams(
            collective_id=0, has_side_effects=True, vmem_limit_bytes=56 * 1024 * 1024
        ),
        cost_estimate=pl.CostEstimate(
            flops=2 * 5 * KEYS * 8 * ROWS * WIDTH,
            bytes_accessed=4 * ROWS * WIDTH * 2 + 3 * ROWS * WIDTH * 4,
            transcendentals=KEYS * 8 * ROWS,
        ),
    )(queries, key_rows, value_rows, out_grad)
    return pl.pallas_call(
        write_out,
        out_shape=(out, out, out),
        in_specs=[near_spec] * 3,
        out_specs=(any_spec,) * 3,
        scratch_shapes=[dma((3,))],
        compiler_params=pltpu.CompilerParams(vmem_limit_bytes=1024*1024),
    )(*grads)


def solution(mesh):
    spec = P(("dp", "ctx"), None)
    return jax.shard_map(
        shards, mesh=mesh, in_specs=(spec,) * 4, out_specs=(spec,) * 3, check_vma=False
    )
```

time: 46.7 us -> 42.1 us (0.901)
  the two profiles are of different devices: /device:TPU:16 before, /device:TPU:1 now
where the time goes in v3:
time: 42.1 us; the launch traced here: 41.9 us
  Pallas kernels  41.3 us (98%)
  between operations  0.64 us (2%)
    pallas_call x1, Pallas kernels, shards(): pl.pallas_call(kernel, out_shape=(near, near, near), in_specs=[any_spec]...  40.5 us

profile of v3, /device:TPU:1, one launch (start us, length us, event | category | flops | bytes accessed | tf_op | source)
XLA Modules:
  0.0 41.9 jit_solution(11676574125660813876)
XLA Ops:
  0.6 40.5 %shard_map.67 = (f32[256,128]{1,0:T(8,128)S(1)}, f32[256,128]{1,0:T(8,128)S(1)}, f32[256,128]{1,0:T(8,128)S(1)}) custom-call(bf16[256,128]{1,0:T(8,128)(2,1)} %q_hbm.1, bf16[256,128]{1,0:T(8,128)(2,1)} %k_hbm.1, bf16[256,128]{1,0:T(8,128)(2,1)} %v_hbm.1, bf16[256,128]{1,0:T(8,128)(2,1)} %g_hbm.1), custom_call_target="tpu_custom_call" | custom-call | flops 2684354560 | bytes 655360 | tf_op jit(solution)/shard_map/pallas_call | solution.py:365
  41.2 0.8 %shard_map.68 = (f32[256,128]{1,0:T(8,128)}, f32[256,128]{1,0:T(8,128)}, f32[256,128]{1,0:T(8,128)}) custom-call(f32[256,128]{1,0:T(8,128)S(1)} %get-tuple-element.6.a_ref, f32[256,128]{1,0:T(8,128)S(1)} %get-tuple-element.7.b_ref, f32[256,128]{1,0:T(8,128)S(1)} %get-tuple-element.8.c_ref), custom_call_target="tpu_custom_call" | custom-call | tf_op jit(solution)/shard_map/pallas_call | solution.py:411

commit v4 on v3

v4 whole, which is shorter than its diff:
```python
import math

import jax
import jax.numpy as jnp
from jax import lax
from jax.experimental import pallas as pl
from jax.experimental.pallas import tpu as pltpu
from jax.sharding import PartitionSpec as P

F32 = jnp.float32
BF16 = jnp.bfloat16
MESH = pl.DeviceIdType.MESH

ROWS = 256
WIDTH = 128
RING = 8
HALF = 512
KEYS = 1024
SCALE = WIDTH ** (-0.5)
EXP2_SCALE = SCALE * math.log2(math.e)

R1, L1, R2, L2, R3, L3, OWN, FAR = range(8)
PLACE = (-1, 1, -2, 2, -3, 3, 0, 4)
SLOT_AT = {p % RING: s for s, p in enumerate(PLACE)}
MIRROR = tuple(SLOT_AT[-p % RING] for p in PLACE)
PEERS = (FAR, R3, L3, R2, L2, R1, L1)
PART = 128

Q_PATH = ((OWN, R1, 1), (OWN, L1, -1), (R1, R2, 1), (L1, L2, -1), (R2, FAR, 2), (R2, R3, 1), (L2, L3, -1))
G_PATH = ((OWN, R1, 1), (OWN, L1, -1), (R1, R2, 1), (L1, L2, -1), (L2, FAR, -2), (R2, R3, 1), (L2, L3, -1))
PIECES = ((0, 2), (2, 0), (1, 3), (3, 1))


def rows_dot(left, right):
    return lax.dot_general(left, right, (((1,), (1,)), ((), ())), preferred_element_type=F32)


def kernel(
    q_hbm, k_hbm, v_hbm, g_hbm,
    dq_out, dk_out, dv_out,
    qbuf, gbuf, kbuf, vbuf, ktbuf, ebuf, dbuf, mbuf,
    part_tx, part_rx, dk_acc, dv_acc,
    dqt, dq_tx, dq_rx, pair_tx, pair_rx, far_tx, far_rx,
    in_sem, gat_send, gat_recv, kv_send, kv_recv, st_send, st_recv,
    dq_send, dq_recv, red_send, red_recv,
):
    me = lax.axis_index("ctx")
    z = me // 4
    w = me % 4
    core = w % 2
    xh = w // 2

    def on_ring(offset):
        return {"ctx": ((z + (offset + RING)) % RING) * 4 + w}

    sibling = {"ctx": z * 4 + xh * 2 + (1 - core)}
    across = {"ctx": z * 4 + (1 - xh) * 2 + core}
    right, left = on_ring(1), on_ring(-1)

    barrier = pltpu.get_barrier_semaphore()
    for peer in (right, left, across, sibling):
        pl.semaphore_signal(barrier, inc=1, device_id=peer, device_id_type=MESH)

    own_rows = pl.ds(0, ROWS)
    loads = [
        pltpu.make_async_copy(src, dst, in_sem.at[i])
        for i, (src, dst) in enumerate(
            (
                (q_hbm.at[pl.ds(0, PART)], qbuf.at[0, OWN]),
                (g_hbm.at[pl.ds(0, PART)], gbuf.at[0, OWN]),
                (q_hbm.at[pl.ds(PART, PART)], qbuf.at[1, OWN]),
                (g_hbm.at[pl.ds(PART, PART)], gbuf.at[1, OWN]),
                (k_hbm, kbuf.at[own_rows]),
                (v_hbm, vbuf.at[own_rows]),
            )
        )
    ]
    for c in loads:
        c.start()
    pending = []

    def send(src, dst, send_sem, recv_sem, peer):
        c = pltpu.make_async_remote_copy(
            src_ref=src, dst_ref=dst, send_sem=send_sem, recv_sem=recv_sem,
            device_id=peer, device_id_type=MESH,
        )
        c.start()
        pending.append(c)
        return c

    for c in loads:
        c.wait()
    pl.semaphore_wait(barrier, 4)

    hops = {}

    def pass_on(piece, slot, way=None):
        buf, path = ((qbuf, Q_PATH), (gbuf, G_PATH))[piece // 2]
        half = piece % 2
        for src, dst, steps in path:
            if src == slot and way in (None, steps > 0):
                n = piece * 8 + dst
                hops[piece, dst] = send(
                    buf.at[half, src], buf.at[half, dst], gat_send.at[n], gat_recv.at[n], on_ring(steps)
                )

    def arrive(piece, slot):
        hops[piece, slot].wait_recv()
        pass_on(piece, slot)

    def key_rows_at(p):
        return pl.ds(p * ROWS, ROWS)

    for a, b in PIECES:
        pass_on(a, OWN, True)
        pass_on(b, OWN, False)
    kv_across = []
    for i, buf in enumerate((kbuf, vbuf)):
        kv_across.append(
            send(buf.at[key_rows_at(0)], buf.at[key_rows_at(2)], kv_send.at[i], kv_recv.at[i], across)
        )
    kv_sibling = []
    for i, buf in enumerate((kbuf, vbuf)):
        kv_sibling.append(
            send(buf.at[key_rows_at(0)], buf.at[key_rows_at(1)], kv_send.at[2 + i], kv_recv.at[2 + i], sibling)
        )
    kv_third = []

    def pass_keys_on():
        for i, buf in enumerate((kbuf, vbuf)):
            kv_across[i].wait_recv()
            kv_third.append(
                send(buf.at[key_rows_at(2)], buf.at[key_rows_at(3)], kv_send.at[4 + i], kv_recv.at[4 + i], sibling)
            )

    def side_by_side(buf, half, pair):
        return buf[half, 2 * pair : 2 * pair + 2].reshape(2 * PART, WIDTH)

    def tile(half, pair):
        t = half * 4 + pair
        queries, grads_out = side_by_side(qbuf, half, pair), side_by_side(gbuf, half, pair)
        for kh in (0, 1):
            keys = pl.ds(kh * HALF, HALF)
            s = rows_dot(kbuf[keys, :], queries)
            m = jnp.max(s, axis=0, keepdims=True)
            e = jnp.exp2((s - m) * EXP2_SCALE)
            ebuf[t, keys, :] = e
            d = rows_dot(vbuf[keys, :], grads_out)
            dbuf[t, keys, :] = d
            mbuf[t, kh, 0:1, :] = m * SCALE
            mbuf[t, kh, 1:2, :] = jnp.sum(e, axis=0, keepdims=True)
            mbuf[t, kh, 2:3, :] = jnp.sum(e * d, axis=0, keepdims=True)
        m0, l0, w0 = (mbuf[t, 0, i : i + 1, :] for i in range(3))
        m1, l1, w1 = (mbuf[t, 1, i : i + 1, :] for i in range(3))
        m = jnp.maximum(m0, m1)
        a0, a1 = jnp.exp(m0 - m), jnp.exp(m1 - m)
        total = l0 * a0 + l1 * a1
        log_total = m + jnp.log(total)
        delta = (w0 * a0 + w1 * a1) / total
        for i in range(2):
            cols = slice(i * PART, (i + 1) * PART)
            part_tx[half, 2 * pair + i, 0:1, :] = log_total[:, cols]
            part_tx[half, 2 * pair + i, 1:2, :] = delta[:, cols]

    st = {}

    def share_stats(half, g):
        group = pl.ds(g * 4, 4)
        n = half * 2 + g
        for slot in PEERS:
            at = MIRROR[slot]
            st[at, half, g] = send(
                part_tx.at[half, group], part_rx.at[at, half, group],
                st_send.at[slot, n], st_recv.at[at, n], on_ring(PLACE[slot]),
            )

    def parts_of(half, t, g):
        found = []
        for u in range(8):
            s = SLOT_AT[(PLACE[t] - PLACE[u]) % RING]
            if s // 4 == g:
                ref = part_tx if u == OWN else part_rx.at[u]
                found.append((ref[half, s, 0:1, :], ref[half, s, 1:2, :]))
        return found

    def combine(parts):
        peak = parts[0][0]
        for part in parts[1:]:
            peak = jnp.maximum(peak, part[0])
        total = jnp.zeros_like(peak)
        weighted = jnp.zeros_like(peak)
        for log_part, delta_part in parts:
            share = jnp.exp(log_part - peak)
            total = total + share
            weighted = weighted + share * delta_part
        return peak + jnp.log(total), weighted / total

    partial = {}

    def early_stats(half):
        for slot in PEERS:
            st[slot, half, 0].wait_recv()
        for slot in range(8):
            partial[half, slot] = combine(parts_of(half, slot, 0))

    def late_stats(half):
        for slot in PEERS:
            st[slot, half, 1].wait_recv()

    rows_stats = {}

    def grads(half, pair, kh):
        t = half * 4 + pair
        if t not in rows_stats:
            both = [combine([partial[half, x]] + parts_of(half, x, 1)) for x in (2 * pair, 2 * pair + 1)]
            rows_stats[t] = tuple(jnp.concatenate(x, axis=1) for x in zip(*both))
        log_total, delta = rows_stats[t]
        keys = pl.ds(kh * HALF, HALF)
        c = jnp.exp(mbuf[t, kh, 0:1, :] - log_total)
        p = ebuf[t, keys, :] * c
        prob_half = p.astype(BF16)
        score_grad = (p * (dbuf[t, keys, :] - delta)).astype(BF16)
        dv = jnp.dot(prob_half, side_by_side(gbuf, half, pair), preferred_element_type=F32)
        dk = jnp.dot(score_grad, side_by_side(qbuf, half, pair), preferred_element_type=F32)
        if (half, pair) == (0, R3 // 2):
            dv_acc[keys, :] = dv
            dk_acc[keys, :] = dk
        else:
            dv_acc[keys, :] += dv
            dk_acc[keys, :] += dk
        return jnp.dot(ktbuf[:, keys], score_grad, preferred_element_type=F32)

    dq = {}
    sides = (slice(0, PART), slice(PART, 2 * PART))
    own_sum, far_sum = (0, 5), (1, 3)

    def send_sum(half, d, kind, value):
        n = (half * 2 + d) * 4 + kind
        dq_tx[n] = value.astype(BF16)
        steps = (4, 1, 2, 1)[kind]
        dq[half, d, kind] = send(
            dq_tx.at[n], dq_rx.at[n], dq_send.at[n], dq_recv.at[n], on_ring(steps if d else -steps)
        )

    def received(half, d, kind):
        dq[half, d, kind].wait_recv()
        return dq_rx[(half * 2 + d) * 4 + kind].astype(F32)

    def send_both(half, kind, value):
        for d in (0, 1):
            send_sum(half, d, kind, value[:, sides[d]])

    def far_sums(half):
        for d in (0, 1):
            send_sum(half, d, 2, dqt[far_sum[half], :, sides[d]] + received(half, d, 1))

    for a, b in PIECES:
        arrive(a, R1)
        arrive(b, L1)
    pass_keys_on()
    for a, b in PIECES[:2]:
        arrive(a, R2)
        arrive(b, L2)
    for c in kv_sibling + kv_third:
        c.wait_recv()
    tile(0, 0)
    for a, b in PIECES[2:]:
        arrive(a, R2)
        arrive(b, L2)
    tile(0, 1)
    tile(1, 0)
    for p in range(4):
        ktbuf[:, p * ROWS : (p + 1) * ROWS] = kbuf[key_rows_at(p), :].astype(F32).T.astype(BF16)
    for half in (0, 1):
        for piece in (half, 2 + half):
            arrive(piece, R3)
            arrive(piece, L3)
        share_stats(half, 0)
        tile(half, 2)
        for piece in (half, 2 + half):
            arrive(piece, FAR)
        tile(half, 3)
        share_stats(half, 1)
        if half == 0:
            tile(1, 1)

    early_stats(0)
    late_stats(0)
    send_both(0, 1, grads(0, 2, 0) + grads(0, 2, 1))
    t = grads(0, 3, 0) + grads(0, 3, 1)
    send_sum(0, 0, 0, t[:, sides[1]])
    dqt[0, :, sides[0]] = t[:, sides[0]]
    dqt[1] = grads(0, 1, 0) + grads(0, 1, 1)
    send_both(0, 3, grads(0, 0, 0) + grads(0, 0, 1))

    early_stats(1)
    late_stats(1)
    send_both(1, 1, grads(1, 2, 0) + grads(1, 2, 1))
    for pair in (3, 1, 0):
        dqt[2 + pair] = grads(1, pair, 1)
    accs = (dk_acc, dv_acc)
    pair_sum = {}
    across_sum = []

    def send_pair(j, p):
        for i, acc in enumerate(accs):
            n = j * 2 + i
            pair_tx[n] = acc[key_rows_at(p), :].astype(BF16)
            pair_sum[j, i] = send(pair_tx.at[n], pair_rx.at[n], red_send.at[n], red_recv.at[n], sibling)

    def from_pair(j, i):
        pair_sum[j, i].wait_recv()
        return pair_rx[j * 2 + i].astype(F32)

    send_pair(0, 3)
    t = dqt[5] + grads(1, 3, 0)
    send_sum(1, 0, 0, t[:, sides[1]])
    dqt[5, :, sides[0]] = t[:, sides[0]]
    far_sums(0)
    dqt[3] += grads(1, 1, 0)
    for i, acc in enumerate(accs):
        far_tx[i] = (acc[key_rows_at(2), :] + from_pair(0, i)).astype(BF16)
        across_sum.append(
            send(far_tx.at[i], far_rx.at[i], red_send.at[4 + i], red_recv.at[4 + i], across)
        )
    send_both(1, 3, dqt[2] + grads(1, 0, 0))
    send_pair(1, 1)
    far_sums(1)

    for half in (0, 1):
        t = dqt[own_sum[half], :, sides[0]] + received(half, 0, 0)
        for d in (0, 1):
            t = t + received(half, d, 3)
        if half == 0:
            for d in (0, 1):
                t = t + received(half, d, 2)
            dq_out[0:PART, :] = t.T * SCALE
        else:
            dqt[5, :, sides[0]] = t
    for i, (acc, out, scale) in enumerate(((dk_acc, dk_out, SCALE), (dv_acc, dv_out, None))):
        t = acc[key_rows_at(0), :] + from_pair(1, i)
        across_sum[i].wait_recv()
        t = t + far_rx[i].astype(F32)
        out[...] = t if scale is None else t * scale
    t = dqt[5, :, sides[0]]
    for d in (0, 1):
        t = t + received(1, d, 2)
    dq_out[PART : 2 * PART, :] = t.T * SCALE
    for c in pending:
        c.wait_send()


def write_out(a_ref, b_ref, c_ref, a_out, b_out, c_out, sems):
    copies = [
        pltpu.make_async_copy(src, dst, sems.at[i])
        for i, (src, dst) in enumerate(((a_ref, a_out), (b_ref, b_out), (c_ref, c_out)))
    ]
    for c in copies:
        c.start()
    for c in copies:
        c.wait()


def shards(queries, key_rows, value_rows, out_grad):
    any_spec = pl.BlockSpec(memory_space=pl.ANY)
    dma = pltpu.SemaphoreType.DMA
    out = jax.ShapeDtypeStruct((ROWS, WIDTH), F32)
    near = pltpu.VMEM((ROWS, WIDTH), F32)
    near_spec = pl.BlockSpec(memory_space=pltpu.VMEM)
    vm = pltpu.VMEM
    grads = pl.pallas_call(
        kernel,
        out_shape=(near, near, near),
        in_specs=[any_spec] * 4,
        out_specs=(near_spec,) * 3,
        scratch_shapes=[
            vm((2, 8, PART, WIDTH), BF16),
            vm((2, 8, PART, WIDTH), BF16),
            vm((KEYS, WIDTH), BF16),
            vm((KEYS, WIDTH), BF16),
            vm((WIDTH, KEYS), BF16),
            vm((8, KEYS, ROWS), F32),
            vm((8, KEYS, ROWS), F32),
            vm((8, 2, 8, ROWS), F32),
            vm((2, 8, 2, PART), F32),
            vm((8, 2, 8, 2, PART), F32),
            vm((KEYS, WIDTH), F32),
            vm((KEYS, WIDTH), F32),
            vm((6, WIDTH, 2 * PART), F32),
            vm((16, WIDTH, PART), BF16),
            vm((16, WIDTH, PART), BF16),
            vm((4, ROWS, WIDTH), BF16),
            vm((4, ROWS, WIDTH), BF16),
            vm((2, ROWS, WIDTH), BF16),
            vm((2, ROWS, WIDTH), BF16),
            dma((6,)),
            dma((32,)),
            dma((32,)),
            dma((6,)),
            dma((6,)),
            dma((8, 4)),
            dma((8, 4)),
            dma((16,)),
            dma((16,)),
            dma((6,)),
            dma((6,)),
        ],
        compiler_params=pltpu.CompilerParams(
            collective_id=0, has_side_effects=True, vmem_limit_bytes=56 * 1024 * 1024
        ),
        cost_estimate=pl.CostEstimate(
            flops=2 * 5 * KEYS * 8 * ROWS * WIDTH,
            bytes_accessed=4 * ROWS * WIDTH * 2 + 3 * ROWS * WIDTH * 4,
            transcendentals=KEYS * 8 * ROWS,
        ),
    )(queries, key_rows, value_rows, out_grad)
    return pl.pallas_call(
        write_out,
        out_shape=(out, out, out),
        in_specs=[near_spec] * 3,
        out_specs=(any_spec,) * 3,
        scratch_shapes=[dma((3,))],
        compiler_params=pltpu.CompilerParams(vmem_limit_bytes=1024*1024),
    )(*grads)


def solution(mesh):
    spec = P(("dp", "ctx"), None)
    return jax.shard_map(
        shards, mesh=mesh, in_specs=(spec,) * 4, out_specs=(spec,) * 3, check_vma=False
    )
```

time: 42.1 us -> 40.3 us (0.957)
  Pallas kernels: 41.3 us -> 39.2 us
    pallas_call x1, Pallas kernels: 40.5 us -> 38.5 us  [shards(): pl.pallas_call(kernel, out_shape=(near, near, near), in_specs=[any_spec]...]
where the time goes in v4:
time: 40.3 us; the launch traced here: 39.9 us
  Pallas kernels  39.2 us (97%)
  between operations  0.64 us (2%)
    pallas_call x1, Pallas kernels, shards(): pl.pallas_call(kernel, out_shape=(near, near, near), in_specs=[any_spec]...  38.5 us

profile of v4, /device:TPU:1, one launch (start us, length us, event | category | flops | bytes accessed | tf_op | source)
XLA Modules:
  0.0 39.9 jit_solution(10023184026672567276)
XLA Ops:
  0.6 38.5 %shard_map.67 = (f32[256,128]{1,0:T(8,128)S(1)}, f32[256,128]{1,0:T(8,128)S(1)}, f32[256,128]{1,0:T(8,128)S(1)}) custom-call(bf16[256,128]{1,0:T(8,128)(2,1)} %q_hbm.1, bf16[256,128]{1,0:T(8,128)(2,1)} %k_hbm.1, bf16[256,128]{1,0:T(8,128)(2,1)} %v_hbm.1, bf16[256,128]{1,0:T(8,128)(2,1)} %g_hbm.1), custom_call_target="tpu_custom_call" | custom-call | flops 2684354560 | bytes 655360 | tf_op jit(solution)/shard_map/pallas_call | solution.py:371
  39.1 0.8 %shard_map.68 = (f32[256,128]{1,0:T(8,128)}, f32[256,128]{1,0:T(8,128)}, f32[256,128]{1,0:T(8,128)}) custom-call(f32[256,128]{1,0:T(8,128)S(1)} %get-tuple-element.6.a_ref, f32[256,128]{1,0:T(8,128)S(1)} %get-tuple-element.7.b_ref, f32[256,128]{1,0:T(8,128)S(1)} %get-tuple-element.8.c_ref), custom_call_target="tpu_custom_call" | custom-call | tf_op jit(solution)/shard_map/pallas_call | solution.py:417

commit v5 on v4

--- a/solution.py
+++ b/solution.py
@@ -136,31 +136,35 @@
     def side_by_side(buf, half, pair):
         return buf[half, 2 * pair : 2 * pair + 2].reshape(2 * PART, WIDTH)
 
-    def tile(half, pair):
+    def tile(half, pair, side=None):
         t = half * 4 + pair
-        queries, grads_out = side_by_side(qbuf, half, pair), side_by_side(gbuf, half, pair)
+        if side is None:
+            cols, slots = slice(0, 2 * PART), (2 * pair, 2 * pair + 1)
+            queries, grads_out = side_by_side(qbuf, half, pair), side_by_side(gbuf, half, pair)
+        else:
+            cols, slots = slice(side * PART, side * PART + PART), (2 * pair + side,)
+            queries, grads_out = qbuf[half, slots[0]], gbuf[half, slots[0]]
         for kh in (0, 1):
             keys = pl.ds(kh * HALF, HALF)
             s = rows_dot(kbuf[keys, :], queries)
             m = jnp.max(s, axis=0, keepdims=True)
             e = jnp.exp2((s - m) * EXP2_SCALE)
-            ebuf[t, keys, :] = e
+            ebuf[t, keys, cols] = e
             d = rows_dot(vbuf[keys, :], grads_out)
-            dbuf[t, keys, :] = d
-            mbuf[t, kh, 0:1, :] = m * SCALE
-            mbuf[t, kh, 1:2, :] = jnp.sum(e, axis=0, keepdims=True)
-            mbuf[t, kh, 2:3, :] = jnp.sum(e * d, axis=0, keepdims=True)
-        m0, l0, w0 = (mbuf[t, 0, i : i + 1, :] for i in range(3))
-        m1, l1, w1 = (mbuf[t, 1, i : i + 1, :] for i in range(3))
+            dbuf[t, keys, cols] = d
+            mbuf[t, kh, 0:1, cols] = m * SCALE
+            mbuf[t, kh, 1:2, cols] = jnp.sum(e, axis=0, keepdims=True)
+            mbuf[t, kh, 2:3, cols] = jnp.sum(e * d, axis=0, keepdims=True)
+        m0, l0, w0 = (mbuf[t, 0, i : i + 1, cols] for i in range(3))
+        m1, l1, w1 = (mbuf[t, 1, i : i + 1, cols] for i in range(3))
         m = jnp.maximum(m0, m1)
         a0, a1 = jnp.exp(m0 - m), jnp.exp(m1 - m)
         total = l0 * a0 + l1 * a1
         log_total = m + jnp.log(total)
         delta = (w0 * a0 + w1 * a1) / total
-        for i in range(2):
-            cols = slice(i * PART, (i + 1) * PART)
-            part_tx[half, 2 * pair + i, 0:1, :] = log_total[:, cols]
-            part_tx[half, 2 * pair + i, 1:2, :] = delta[:, cols]
+        for i, slot in enumerate(slots):
+            part_tx[half, slot, 0:1, :] = log_total[:, i * PART : (i + 1) * PART]
+            part_tx[half, slot, 1:2, :] = delta[:, i * PART : (i + 1) * PART]
 
     st = {}
 
@@ -263,11 +267,13 @@
         arrive(b, L2)
     for c in kv_sibling + kv_third:
         c.wait_recv()
+    tile(0, 3, 0)
     tile(0, 0)
     for a, b in PIECES[2:]:
         arrive(a, R2)
         arrive(b, L2)
     tile(0, 1)
+    tile(1, 3, 0)
     tile(1, 0)
     for p in range(4):
         ktbuf[:, p * ROWS : (p + 1) * ROWS] = kbuf[key_rows_at(p), :].astype(F32).T.astype(BF16)
@@ -275,14 +281,16 @@
         for piece in (half, 2 + half):
             arrive(piece, R3)
             arrive(piece, L3)
-        share_stats(half, 0)
+        if half == 0:
+            share_stats(0, 0)
         tile(half, 2)
         for piece in (half, 2 + half):
             arrive(piece, FAR)
-        tile(half, 3)
+        tile(half, 3, 1)
         share_stats(half, 1)
         if half == 0:
             tile(1, 1)
+            share_stats(1, 0)
 
     early_stats(0)
     late_stats(0)
@@ -295,7 +303,7 @@
 
     early_stats(1)
     late_stats(1)
-    send_both(1, 1, grads(1, 2, 0) + grads(1, 2, 1))
+    dqt[4] = grads(1, 2, 1)
     for pair in (3, 1, 0):
         dqt[2 + pair] = grads(1, pair, 1)
     accs = (dk_acc, dv_acc)
@@ -313,6 +321,7 @@
         return pair_rx[j * 2 + i].astype(F32)
 
     send_pair(0, 3)
+    send_both(1, 1, dqt[4] + grads(1, 2, 0))
     t = dqt[5] + grads(1, 3, 0)
     send_sum(1, 0, 0, t[:, sides[1]])
     dqt[5, :, sides[0]] = t[:, sides[0]]

time: 40.3 us -> 39.6 us (0.983)
    pallas_call x1, Pallas kernels: 38.5 us -> 38 us  [shards(): pl.pallas_call(kernel, out_shape=(near, near, near), in_specs=[any_spec]...]
where the time goes in v5:
time: 39.6 us; the launch traced here: 39.4 us
  Pallas kernels  38.8 us (98%)
  between operations  0.64 us (2%)
    pallas_call x1, Pallas kernels, shards(): pl.pallas_call(kernel, out_shape=(near, near, near), in_specs=[any_spec]...  38 us

profile of v5, /device:TPU:1, one launch (start us, length us, event | category | flops | bytes accessed | tf_op | source)
XLA Modules:
  0.0 39.4 jit_solution(15420314144908581859)
XLA Ops:
  0.6 38.0 %shard_map.67 = (f32[256,128]{1,0:T(8,128)S(1)}, f32[256,128]{1,0:T(8,128)S(1)}, f32[256,128]{1,0:T(8,128)S(1)}) custom-call(bf16[256,128]{1,0:T(8,128)(2,1)} %q_hbm.1, bf16[256,128]{1,0:T(8,128)(2,1)} %k_hbm.1, bf16[256,128]{1,0:T(8,128)(2,1)} %v_hbm.1, bf16[256,128]{1,0:T(8,128)(2,1)} %g_hbm.1), custom_call_target="tpu_custom_call" | custom-call | flops 2684354560 | bytes 655360 | tf_op jit(solution)/shard_map/pallas_call | solution.py:380
  38.7 0.8 %shard_map.68 = (f32[256,128]{1,0:T(8,128)}, f32[256,128]{1,0:T(8,128)}, f32[256,128]{1,0:T(8,128)}) custom-call(f32[256,128]{1,0:T(8,128)S(1)} %get-tuple-element.6.a_ref, f32[256,128]{1,0:T(8,128)S(1)} %get-tuple-element.7.b_ref, f32[256,128]{1,0:T(8,128)S(1)} %get-tuple-element.8.c_ref), custom_call_target="tpu_custom_call" | custom-call | tf_op jit(solution)/shard_map/pallas_call | solution.py:426

commit v6 on v5

--- a/solution.py
+++ b/solution.py
@@ -275,8 +275,6 @@
     tile(0, 1)
     tile(1, 3, 0)
     tile(1, 0)
-    for p in range(4):
-        ktbuf[:, p * ROWS : (p + 1) * ROWS] = kbuf[key_rows_at(p), :].astype(F32).T.astype(BF16)
     for half in (0, 1):
         for piece in (half, 2 + half):
             arrive(piece, R3)
@@ -292,6 +290,8 @@
             tile(1, 1)
             share_stats(1, 0)
 
+    for p in range(4):
+        ktbuf[:, p * ROWS : (p + 1) * ROWS] = kbuf[key_rows_at(p), :].astype(F32).T.astype(BF16)
     early_stats(0)
     late_stats(0)
     send_both(0, 1, grads(0, 2, 0) + grads(0, 2, 1))

time: 39.6 us -> 39.6 us (level)
  no operation moved by 1% of the time
where the time goes in v6:
time: 39.6 us; the launch traced here: 39.4 us
  Pallas kernels  38.8 us (98%)
  between operations  0.64 us (2%)
    pallas_call x1, Pallas kernels, shards(): pl.pallas_call(kernel, out_shape=(near, near, near), in_specs=[any_spec]...  38 us

profile of v6, /device:TPU:1, one launch (start us, length us, event | category | flops | bytes accessed | tf_op | source)
XLA Modules:
  0.0 39.4 jit_solution(2661569719344662675)
XLA Ops:
  0.6 38.0 %shard_map.67 = (f32[256,128]{1,0:T(8,128)S(1)}, f32[256,128]{1,0:T(8,128)S(1)}, f32[256,128]{1,0:T(8,128)S(1)}) custom-call(bf16[256,128]{1,0:T(8,128)(2,1)} %q_hbm.1, bf16[256,128]{1,0:T(8,128)(2,1)} %k_hbm.1, bf16[256,128]{1,0:T(8,128)(2,1)} %v_hbm.1, bf16[256,128]{1,0:T(8,128)(2,1)} %g_hbm.1), custom_call_target="tpu_custom_call" | custom-call | flops 2684354560 | bytes 655360 | tf_op jit(solution)/shard_map/pallas_call | solution.py:380
  38.7 0.8 %shard_map.68 = (f32[256,128]{1,0:T(8,128)}, f32[256,128]{1,0:T(8,128)}, f32[256,128]{1,0:T(8,128)}) custom-call(f32[256,128]{1,0:T(8,128)S(1)} %get-tuple-element.6.a_ref, f32[256,128]{1,0:T(8,128)S(1)} %get-tuple-element.7.b_ref, f32[256,128]{1,0:T(8,128)S(1)} %get-tuple-element.8.c_ref), custom_call_target="tpu_custom_call" | custom-call | tf_op jit(solution)/shard_map/pallas_call | solution.py:426

commit v7 on v6

--- a/solution.py
+++ b/solution.py
@@ -273,7 +273,6 @@
         arrive(a, R2)
         arrive(b, L2)
     tile(0, 1)
-    tile(1, 3, 0)
     tile(1, 0)
     for half in (0, 1):
         for piece in (half, 2 + half):
@@ -287,6 +286,7 @@
         tile(half, 3, 1)
         share_stats(half, 1)
         if half == 0:
+            tile(1, 3, 0)
             tile(1, 1)
             share_stats(1, 0)
 

time: 39.6 us -> 39.5 us (level)
  no operation moved by 1% of the time
where the time goes in v7:
time: 39.5 us; the launch traced here: 39.4 us
  Pallas kernels  38.8 us (98%)
  between operations  0.64 us (2%)
    pallas_call x1, Pallas kernels, shards(): pl.pallas_call(kernel, out_shape=(near, near, near), in_specs=[any_spec]...  38 us

profile of v7, /device:TPU:1, one launch (start us, length us, event | category | flops | bytes accessed | tf_op | source)
XLA Modules:
  0.0 39.4 jit_solution(15661345662721651725)
XLA Ops:
  0.6 38.0 %shard_map.67 = (f32[256,128]{1,0:T(8,128)S(1)}, f32[256,128]{1,0:T(8,128)S(1)}, f32[256,128]{1,0:T(8,128)S(1)}) custom-call(bf16[256,128]{1,0:T(8,128)(2,1)} %q_hbm.1, bf16[256,128]{1,0:T(8,128)(2,1)} %k_hbm.1, bf16[256,128]{1,0:T(8,128)(2,1)} %v_hbm.1, bf16[256,128]{1,0:T(8,128)(2,1)} %g_hbm.1), custom_call_target="tpu_custom_call" | custom-call | flops 2684354560 | bytes 655360 | tf_op jit(solution)/shard_map/pallas_call | solution.py:380
  38.6 0.8 %shard_map.68 = (f32[256,128]{1,0:T(8,128)}, f32[256,128]{1,0:T(8,128)}, f32[256,128]{1,0:T(8,128)}) custom-call(f32[256,128]{1,0:T(8,128)S(1)} %get-tuple-element.6.a_ref, f32[256,128]{1,0:T(8,128)S(1)} %get-tuple-element.7.b_ref, f32[256,128]{1,0:T(8,128)S(1)} %get-tuple-element.8.c_ref), custom_call_target="tpu_custom_call" | custom-call | tf_op jit(solution)/shard_map/pallas_call | solution.py:426
